TPU v7x, 256 devices: a whole 4x4x8 slice. The times are simulated.
256 devices in a mesh: dp: 64 (over y, z, core), sp: 4 (over x).
Axes of the slice: x: 4, y: 4, z: 8, core: 2. Of those that a mesh axis runs over, the one named last changes fastest.
Arguments:
- normed: bfloat16 [32768, 2560], P(('dp', 'sp')), may hold values from -24 to 24
- w_query: bfloat16 [2560, 4096], P(None, 'sp'), may hold values from -0.125 to 0.125
- key_weight: bfloat16 [2560, 512], P(None, 'sp'), may hold values from -0.125 to 0.125
- value_weight: bfloat16 [2560, 512], P(None, 'sp'), may hold values from -0.125 to 0.125
- q_gain: float32 [128], replicated, may hold values from 0.25 to 1.75
- key_norm_gain: float32 [128], replicated, may hold values from 0.25 to 1.75
- ctx_grad: bfloat16 [32768, 4096], P(('dp', 'sp')), may hold values from -6 to 6
- lengths: int32 [64], P('dp'), may hold values from 64 to 512, as said below
Outputs:
- normed_input_gradient: bfloat16 [32768, 2560], P(('dp', 'sp'))
- grad_w_query: float32 [2560, 4096], P('dp', 'sp')
- grad_w_key: float32 [2560, 512], P('dp', 'sp')
- grad_w_value: float32 [2560, 512], P('dp', 'sp')
Inputs may be any that keep to these rules, and one draw needn't show every extreme that they name: `lengths`: in every draw some response has its whole span valid and some only one eighth of 512.
All inputs are finite; a program needn't handle non-finite values.
Results may differ from a plain program's by a relative error of at most 0.008.
Values may be sent and summed in bfloat16 or wider, within the bound.
A program may use at most 128 MiB of HBM per device.

v0:
```python
import math

import jax
import jax.numpy as jnp
from jax import lax
from jax.sharding import PartitionSpec as P

epsilon = 1e-06
log_base = math.log(1000000.0)


def angle_tables(length, width):
    position = jnp.arange(length, dtype=jnp.int32).astype(jnp.float32)
    freqs = jnp.exp(jnp.arange(width // 2, dtype=jnp.float32) * (-2.0 * log_base / width))
    angles = position[:, None] * freqs[None, :]
    cosine_table = jnp.cos(angles)
    sine_values = jnp.sin(angles)
    return (
        jnp.concatenate([cosine_table, cosine_table], 1),
        jnp.concatenate([sine_values, sine_values], 1),
    )


def turned(values):
    half = values.shape[-1] // 2
    return jnp.concatenate([-values[..., half:], values[..., :half]], -1)


def rotate_pairs(values, cosine_table, sine_values):
    return values * cosine_table + turned(values) * sine_values


def inverse_rotation(grads, cosine_table, sine_values):
    return grads * cosine_table - turned(grads) * sine_values


def normalize(values, gain):
    inverse = lax.rsqrt(jnp.mean(values * values, -1, keepdims=True) + epsilon)
    return (values * inverse * gain, inverse)


def head_norm_gradient(values, inverse, gain, grads):
    weighted = gain * grads
    return inverse * weighted - values * (inverse * inverse * inverse) * jnp.mean(
        values * weighted, -1, keepdims=True
    )


def column_product(span, grads):
    return lax.dot_general(
        span, grads, (((0,), (0,)), ((), ())), preferred_element_type=jnp.float32
    )


def local(normed, w_query, key_weight, value_weight, q_gain, key_norm_gain, ctx_grad, lengths):
    span = lax.all_gather(normed, "sp", axis=0, tiled=True)
    length = span.shape[0]
    head_dim = q_gain.shape[0]
    query_heads = w_query.shape[1] // head_dim
    pair_heads = key_weight.shape[1] // head_dim
    group_size = query_heads // pair_heads
    scale_factor = head_dim ** (-0.5)
    cosine_table, sine_values = angle_tables(length, head_dim)
    q_proj = jnp.dot(span, w_query, preferred_element_type=jnp.float32).reshape(
        length, query_heads, head_dim
    )
    key_projected = jnp.dot(span, key_weight, preferred_element_type=jnp.float32).reshape(
        length, pair_heads, head_dim
    )
    value_row_block = (
        jnp.dot(span, value_weight, preferred_element_type=jnp.float32)
        .astype(jnp.bfloat16)
        .reshape(length, pair_heads, head_dim)
    )
    q_normed, q_inverse = normalize(q_proj, q_gain)
    k_normed, key_inverse_norm = normalize(key_projected, key_norm_gain)
    query_matrix = rotate_pairs(q_normed, cosine_table[:, None, :], sine_values[:, None, :]).astype(
        jnp.bfloat16
    )
    key_rows = rotate_pairs(k_normed, cosine_table[:, None, :], sine_values[:, None, :]).astype(
        jnp.bfloat16
    )
    output_gradient = lax.all_to_all(ctx_grad, "sp", split_axis=1, concat_axis=0, tiled=True)
    positions = jnp.arange(length, dtype=jnp.int32)
    unmasked_rows = positions < lengths[0]
    output_gradient = jnp.where(
        unmasked_rows[:, None], output_gradient, jnp.zeros((), jnp.bfloat16)
    ).reshape(length, query_heads, head_dim)
    allowed = (positions[None, :] <= positions[:, None]) & unmasked_rows[None, :]
    key_sums = [jnp.zeros((length, head_dim), jnp.float32)]
    value_sums = [jnp.zeros((length, head_dim), jnp.float32)]
    query_parts = []
    for head_index in range(query_heads):
        pair_index = head_index // group_size
        q_head = query_matrix[:, head_index]
        k_head = key_rows[:, pair_index]
        v_head = value_row_block[:, pair_index]
        o_grad = output_gradient[:, head_index]
        scores = (
            lax.dot_general(
                q_head, k_head, (((1,), (1,)), ((), ())), preferred_element_type=jnp.float32
            )
            * scale_factor
        )
        weights = jnp.where(allowed, jnp.exp(scores), jnp.zeros((), jnp.float32))
        probs = weights / jnp.sum(weights, -1, keepdims=True)
        probabilities_reduced = probs.astype(jnp.bfloat16)
        context = jnp.dot(probabilities_reduced, v_head, preferred_element_type=jnp.float32)
        delta = jnp.sum(o_grad.astype(jnp.float32) * context, -1, keepdims=True)
        dprob = lax.dot_general(
            o_grad, v_head, (((1,), (1,)), ((), ())), preferred_element_type=jnp.float32
        )
        dscore = (probs * (dprob - delta)).astype(jnp.bfloat16)
        dq_rot = jnp.dot(dscore, k_head, preferred_element_type=jnp.float32) * scale_factor
        key_sums[pair_index] = (
            key_sums[pair_index]
            + lax.dot_general(
                dscore, q_head, (((0,), (0,)), ((), ())), preferred_element_type=jnp.float32
            )
            * scale_factor
        )
        value_sums[pair_index] = value_sums[pair_index] + lax.dot_general(
            probabilities_reduced,
            o_grad,
            (((0,), (0,)), ((), ())),
            preferred_element_type=jnp.float32,
        )
        head_grad = head_norm_gradient(
            q_proj[:, head_index],
            q_inverse[:, head_index],
            q_gain,
            inverse_rotation(dq_rot, cosine_table, sine_values),
        ).astype(jnp.bfloat16)
        query_parts.append(head_grad)
    query_grad = jnp.stack(query_parts, 1).reshape(length, query_heads * head_dim)
    rotated_key_gradient = jnp.stack(key_sums, 1)
    key_gradient = (
        head_norm_gradient(
            key_projected,
            key_inverse_norm,
            key_norm_gain,
            inverse_rotation(
                rotated_key_gradient, cosine_table[:, None, :], sine_values[:, None, :]
            ),
        )
        .astype(jnp.bfloat16)
        .reshape(length, pair_heads * head_dim)
    )
    value_gradient = (
        jnp.stack(value_sums, 1).astype(jnp.bfloat16).reshape(length, pair_heads * head_dim)
    )
    total = lax.dot_general(
        query_grad, w_query, (((1,), (1,)), ((), ())), preferred_element_type=jnp.float32
    )
    total = total + lax.dot_general(
        key_gradient, key_weight, (((1,), (1,)), ((), ())), preferred_element_type=jnp.float32
    )
    normed_input_gradient = lax.psum_scatter(
        total
        + lax.dot_general(
            value_gradient,
            value_weight,
            (((1,), (1,)), ((), ())),
            preferred_element_type=jnp.float32,
        ),
        "sp",
        scatter_dimension=0,
        tiled=True,
    ).astype(jnp.bfloat16)
    pair_width = pair_heads * head_dim
    all_grads = jnp.concatenate([query_grad, key_gradient, value_gradient], 1)
    everything = lax.psum_scatter(
        column_product(span, all_grads), "dp", scatter_dimension=0, tiled=True
    )
    query_width = query_heads * head_dim
    grad_w_query = everything[:, :query_width]
    grad_w_key = everything[:, query_width : query_width + pair_width]
    grad_w_value = everything[:, query_width + pair_width :]
    return (normed_input_gradient, grad_w_query, grad_w_key, grad_w_value)


def solution(mesh):
    in_specs = (
        P(("dp", "sp"), None),
        P(None, "sp"),
        P(None, "sp"),
        P(None, "sp"),
        P(),
        P(),
        P(("dp", "sp"), None),
        P("dp"),
    )
    out_specs = (P(("dp", "sp"), None), P("dp", "sp"), P("dp", "sp"), P("dp", "sp"))
    return jax.shard_map(local, mesh=mesh, in_specs=in_specs, out_specs=out_specs, check_vma=False)
```

profile of v0, /device:TPU:1, one launch (start us, length us, event | category | flops | bytes accessed | tf_op | source)
XLA Modules:
  0.0 351.5 jit_solution(9655931443951024852)
XLA Ops:
  7.9 2.3 copy.86
  10.2 4.8 %all-to-all-start = ((bf16[128,4,1024]{0,2,1:T(8,128)(2,1)}), bf16[128,4,1024]{0,2,1:T(8,128)(2,1)S(1)}, u32[]{:S(2)}, u32[]{:S(2)}) async-start(bf16[128,4,1024]{0,2,1:T(8,128)(2,1)} %bitcast.7), calls=%async_computation | async-start | bytes 2097152 | tf_op jit(solution)/shard_map/all_to_all | solution.py:83
  16.2 12.0 %all-to-all-done = bf16[128,4,1024]{0,2,1:T(8,128)(2,1)S(1)} async-done(((bf16[128,4,1024]{0,2,1:T(8,128)(2,1)}), bf16[128,4,1024]{0,2,1:T(8,128)(2,1)S(1)}, u32[]{:S(2)}, u32[]{:S(2)}) %all-to-all-start) | async-done | bytes 1048608 | tf_op jit(solution)/shard_map/all_to_all | solution.py:83
  30.6 21.5 %all-gather.2.cloned.1.call-done = bf16[512,2560]{1,0:T(8,128)(2,1)} async-done(((bf16[128,2560]{1,0:T(8,128)(2,1)}), bf16[512,2560]{1,0:T(8,128)(2,1)}) %all-gather.2.cloned.1.call-update) | async-done | bytes 2621456 | tf_op jit(solution)/shard_map/all_gather | solution.py:56
  52.1 5.6 %fusion.168 = f32[512,1024]{1,0:T(8,128)S(1)} fusion(bf16[512,2560]{1,0:T(8,128)(2,1)} %all-gather.2.cloned.1.call-done, bf16[2560,1024]{1,0:T(8,128)(2,1)} %param.9), kind=kOutput, calls=%fused_computation.293 | convolution fusion | flops 2684354560 | bytes 9961472 | tf_op jit(solution)/shard_map/dot_general | solution.py:64
  58.2 1.3 multiply_reduce_fusion
  59.5 2.5 fusion.157
  64.0 1.8 copy.84
  65.8 1.8 copy.85
  70.4 1.4 fusion.2
  71.9 1.4 fusion.160
  73.3 1.4 fusion.162
  74.7 1.5 fusion.164
  76.2 1.4 fusion.166
  77.6 1.4 fusion.167
  79.0 1.4 fusion.165
  80.4 1.4 fusion.163
  82.3 2.2 fusion.131
  85.3 1.2 fusion.42
  86.6 1.2 fusion.39
  90.0 1.1 copy.118
  93.0 1.7 fusion.49
  113.6 3.0 fusion.169
  117.8 3.3 add_add_fusion
  121.2 1.1 copy-done.21
  122.3 9.4 %convolution_bitcast_fusion = f32[2560,1280]{0,1:T(8,128)} fusion(bf16[512,2560]{1,0:T(8,128)(2,1)} %all-gather.2.cloned.1.call-done, bf16[512,128]{0,1:T(8,128)(2,1)S(1)} %fusion.41, bf16[512,128]{0,1:T(8,128)(2,1)S(1)} %subtract_convert_fusion, bf16[512,1024]{0,1:T(8,128)(2,1)S(1)} %bitcast.377), kind=kOutput, calls=%fused_computation | convolution fusion | flops 3359375360 | bytes 17039360 | tf_op jit(solution)/shard_map/dot_general | solution.py:50
  131.7 14.0 %copy.115 = f32[2560,1280]{1,0:T(8,128)} copy(f32[2560,1280]{0,1:T(8,128)} %convolution_bitcast_fusion) | data formatting | bytes 26214400
  145.8 34.4 %reduce-scatter.5.cloned.1.call-done = f32[128,2560]{1,0:T(8,128)} async-done(((f32[512,2560]{1,0:T(8,128)}), f32[128,2560]{1,0:T(8,128)}) %reduce-scatter.5.cloned.1.call-update) | async-done | bytes 1310736 | tf_op jit(solution)/shard_map/reduce_scatter | solution.py:158
  180.1 2.2 convert_element_type.168
  182.4 159.7 %reduce-scatter.7.cloned.1.call-done = f32[40,1280]{1,0:T(8,128)} async-done(((f32[2560,1280]{1,0:T(8,128)}), f32[40,1280]{1,0:T(8,128)}) %reduce-scatter.7.cloned.1.call-update) | async-done | bytes 204816
  342.1 1.4 fusion.158
  343.4 1.6 slice.282
  (175 shorter events, 33.8 us)
Async XLA Ops:
  7.2 54.8 %copy-start = (bf16[2560,128]{1,0:T(8,128)(2,1)S(1)}, bf16[2560,128]{1,0:T(8,128)(2,1)}, u32[]{:S(2)}) copy-start(bf16[2560,128]{1,0:T(8,128)(2,1)} %param.10) | copy-start | bytes 1966084
  7.2 44.9 %all-gather.2.cloned.1.call-start = ((), (), s32[]{:S(2)}) async-start(), calls=%async_computation.3 | async-start | bytes 3276800 | tf_op jit(solution)/shard_map/all_gather | solution.py:56
  10.2 18.1 %all-to-all-start = ((bf16[128,4,1024]{0,2,1:T(8,128)(2,1)}), bf16[128,4,1024]{0,2,1:T(8,128)(2,1)S(1)}, u32[]{:S(2)}, u32[]{:S(2)}) async-start(bf16[128,4,1024]{0,2,1:T(8,128)(2,1)} %bitcast.7), calls=%async_computation | async-start | bytes 2097152 | tf_op jit(solution)/shard_map/all_to_all | solution.py:83
  15.0 165.1 %reduce-scatter.5.cloned.1.call-start = ((), (), s32[]{:S(2)}) async-start(), calls=%async_computation.4 | async-start | bytes 6553600 | tf_op jit(solution)/shard_map/reduce_scatter | solution.py:158
  59.5 2.5 copy-start.3
  63.0 5.6 %copy-start.19 = (f32[128]{0:T(128)S(1)}, f32[128]{0:T(128)}, u32[]{:S(2)}) copy-start(f32[128]{0:T(128)} %param.12) | copy-start | bytes 1540
  71.9 16.2 %copy-start.1 = (bf16[512,8,128]{2,0,1:T(8,128)(2,1)}, bf16[512,8,128]{2,0,1:T(8,128)(2,1)S(1)}, u32[]{:S(2)}) copy-start(bf16[512,8,128]{2,0,1:T(8,128)(2,1)S(1)} %fusion.2) | copy-start | bytes 3145732
  81.8 2.7 copy-start.4
  81.8 2.7 copy-start.16
  85.3 1.3 copy-start.23
  86.6 2.6 copy-start.12
  87.8 1.6 copy-start.11
  87.8 1.7 copy-start.10
  87.8 1.8 copy-start.9
  87.8 2.0 copy-start.8
  88.1 2.9 copy-start.7
  93.0 1.8 copy-start.6
  93.0 1.8 copy-start.24
  93.0 2.0 copy-start.25
  95.0 1.2 copy-start.26
  96.5 1.2 copy-start.27
  98.0 1.2 copy-start.28
  99.5 1.2 copy-start.29
  101.0 1.2 copy-start.30
  102.6 1.2 copy-start.31
  106.9 1.2 copy-start.2
  107.0 1.3 copy-start.15
  110.9 2.3 slice-start
  111.8 1.8 slice-start.1
  112.8 3.8 %copy-start.20 = (bf16[512,8,128]{0,2,1:T(8,128)(2,1)}, bf16[512,8,128]{0,2,1:T(8,128)(2,1)S(1)}, u32[]{:S(2)}) copy-start(bf16[512,8,128]{0,2,1:T(8,128)(2,1)S(1)} %fusion.127) | copy-start | bytes 3145732
  121.1 1.2 copy-start.21
  121.1 221.0 %reduce-scatter.7.cloned.1.call-start = ((), (), s32[]{:S(2)}) async-start(), calls=%async_computation.5 | async-start | bytes 13312000
  (6 other events, 6.0 us)
Sparse Core Ops, SparseCore 0:
  9.8 42.2 all-gather.1
  121.2 58.8 reduce-scatter.4
  184.5 157.5 reduce-scatter.6
where the time goes:
time: 356 us; the launch traced here: 352 us
  waiting for transfers between devices  228 us (64%)
  matrix products  51.6 us (14%)
  local copies, waits for them, and re-layouts  40.3 us (11%)
  between operations  15.3 us (4%)
  other arithmetic  11.1 us (3%)
  starting transfers between devices  4.92 us (1%)
    unnamed x4, waiting for transfers between devices  160 us
    reduce_scatter x1, waiting for transfers between devices, local(): lax.psum_scatter(total + lax.dot_general(value_gradient, value_weight, ((...  34.4 us
    unnamed x79, local copies, waits for them, and re-layouts  29 us
    all_gather x1, waiting for transfers between devices, local(): span = lax.all_gather(normed, 'sp', axis=0, tiled=True)  21.5 us
    all_to_all x1, waiting for transfers between devices, local(): lax.all_to_all(ctx_grad, 'sp', split_axis=1, concat_axis=0, tiled=True)  12 us
    dot_general x8, matrix products, local(): lax.dot_general(q_head, k_head, (((1,), (1,)), ((), ())), preferred_eleme...  10.3 us
    dot_general x1, matrix products, column_product(): lax.dot_general(span, grads, (((0,), (0,)), ((), ())), preferred_element_...  9.37 us
  transfers between devices with their start and end apart: 4, of which 4 were waited for; matrix products, arithmetic and copies ran while one was open for 9% of the time, Pallas kernels for 0%

commit v1 on v0

v1 whole, which is shorter than its diff:
```python
import math

import jax
import jax.numpy as jnp
import numpy as np
from jax import lax
from jax.experimental import pallas as pl
from jax.experimental.pallas import tpu as pltpu
from jax.sharding import PartitionSpec as P

F32 = jnp.float32
BF16 = jnp.bfloat16
EPSILON = 1e-06
LOG_BASE = math.log(1000000.0)
RING_X, RING_Y, RING_Z = 4, 4, 8
ROWS = 128
SPAN = 512
FEATURES = 2560
HEADS = 8
HEAD = 128
QUERY_COLUMNS = HEADS * HEAD
COLUMNS = QUERY_COLUMNS + 2 * HEAD
PAIR = 2 * HEAD
TILES = COLUMNS // PAIR
BLOCKS = RING_Y * RING_Z
BLOCK_ROWS = FEATURES // BLOCKS
SHARE = BLOCK_ROWS // 2
SCALE = HEAD**-0.5
SCORE_SCALE = SCALE * math.log2(math.e)
QUERY_ROWS = 256

GATHER = 0
CONTEXT = GATHER + 6
CORE = CONTEXT + 3 * (TILES - 1)
Y_SLOT = CORE + TILES
Z_SLOT = Y_SLOT + 6 * TILES
FINAL = Z_SLOT + 7 * TILES
INPUT = FINAL + 1
SLOTS = INPUT + 6


def angle_tables():
    position = np.arange(SPAN, dtype=np.float32)
    freqs = np.exp(np.arange(HEAD // 2, dtype=np.float32) * np.float32(-2.0 * LOG_BASE / HEAD))
    angles = position[:, None] * freqs.astype(np.float32)[None, :]
    cosine, sine = np.cos(angles), np.sin(angles)
    return (
        np.concatenate([cosine, cosine], 1).astype(np.float32),
        np.concatenate([-sine, sine], 1).astype(np.float32),
    )


def dot(a, b):
    return jnp.dot(a, b, preferred_element_type=F32)


def dot_t(a, b):
    return lax.dot_general(a, b, (((1,), (1,)), ((), ())), preferred_element_type=F32)


def half_turn(a):
    return pltpu.roll(a, HEAD // 2, 1)


def head_mean(a):
    return jnp.sum(a, -1, keepdims=True) * (1.0 / HEAD)


def aligned(index, unit):
    return pl.multiple_of(index * unit, unit)


def kernel(
    normed, w_query, key_weight, value_weight, q_gain, k_gain, ctx_in, lengths, cosine, sine,
    dx_out, gq_out, gk_out, gv_out,
    weights, span, span_t, ctx, u_query, u_key, queries, queries_t, keys, values,
    grads, dk_t, dv_t,
    part, part_send, part_recv, y_far_r, y_far_l, y_near_r, y_near_l,
    z_total, z_send_r, z_send_l, z_recv_r, z_recv_l, result, result_recv,
    dx_far, dx_send_r, dx_send_l, dx_wait_r, dx_wait_l, dx_own,
    x_far_r, x_far_l, x_near_r, x_near_l,
    local_sem, send_sem, recv_sem,
):
    dp = lax.axis_index("dp")
    x = lax.axis_index("sp")
    core = lax.rem(dp, 2)
    z = lax.rem(lax.div(dp, 2), RING_Z)
    y = lax.div(dp, 2 * RING_Z)

    def place(y_at, z_at, core_at):
        return (y_at * RING_Z + z_at) * 2 + core_at

    x_next, x_prev, x_far = lax.rem(x + 1, RING_X), lax.rem(x + 3, RING_X), lax.rem(x + 2, RING_X)
    y_next, y_prev, y_far = lax.rem(y + 1, RING_Y), lax.rem(y + 3, RING_Y), lax.rem(y + 2, RING_Y)
    z_next, z_prev = lax.rem(z + 1, RING_Z), lax.rem(z + RING_Z - 1, RING_Z)
    to_xr, to_xl, to_xf = (dp, x_next), (dp, x_prev), (dp, x_far)
    to_yr, to_yl = (place(y_next, z, core), x), (place(y_prev, z, core), x)
    to_zr, to_zl = (place(y, z_next, core), x), (place(y, z_prev, core), x)
    to_core = (place(y, z, 1 - core), x)

    def remote(src, dst, slot, device):
        return pltpu.make_async_remote_copy(
            src_ref=src,
            dst_ref=dst,
            send_sem=send_sem.at[slot],
            recv_sem=recv_sem.at[slot],
            device_id=device,
            device_id_type=pl.DeviceIdType.MESH,
        )

    own_rows = pltpu.make_async_copy(normed, span.at[x], local_sem.at[0])
    own_weights = [
        pltpu.make_async_copy(w_query, weights.at[:, pl.ds(0, QUERY_COLUMNS)], local_sem.at[1]),
        pltpu.make_async_copy(
            key_weight, weights.at[:, pl.ds(QUERY_COLUMNS, HEAD)], local_sem.at[2]
        ),
        pltpu.make_async_copy(
            value_weight, weights.at[:, pl.ds(QUERY_COLUMNS + HEAD, HEAD)], local_sem.at[3]
        ),
    ]
    own_context = pltpu.make_async_copy(
        ctx_in.at[:, pl.ds(aligned(x, QUERY_COLUMNS), QUERY_COLUMNS)],
        ctx.at[pl.ds(aligned(x, ROWS), ROWS), :],
        local_sem.at[4],
    )
    own_rows.start()
    for copy in own_weights:
        copy.start()
    own_context.start()

    barrier = pltpu.get_barrier_semaphore()
    for device in (to_xr, to_xl, to_xf, to_yr, to_yl, to_zr, to_zl, to_core):
        pl.semaphore_signal(barrier, inc=1, device_id=device, device_id_type=pl.DeviceIdType.MESH)
    pl.semaphore_wait(barrier, 8)

    low, high = pl.ds(0, ROWS // 2), pl.ds(ROWS // 2, ROWS // 2)

    def gather_own(slot, half, device):
        return remote(normed.at[half, :], span.at[x, half, :], GATHER + slot, device)

    def gather_pass(slot, owner, half, device):
        return remote(
            span.at[owner, half, :], span.at[owner, half, :], GATHER + slot, device
        )

    right_low, right_high = gather_own(0, low, to_xr), gather_own(1, high, to_xr)
    left_high, left_low = gather_own(2, high, to_xl), gather_own(3, low, to_xl)
    pass_right = gather_pass(4, x_prev, low, to_xr)
    pass_left = gather_pass(5, x_next, high, to_xl)
    right_low.start()
    left_high.start()
    right_high.start()
    left_low.start()

    def context_copy(tile, slot, owner, device):
        start = pl.multiple_of(owner * QUERY_COLUMNS + tile * PAIR, PAIR)
        return remote(
            ctx_in.at[:, pl.ds(start, PAIR)],
            ctx.at[pl.ds(aligned(x, ROWS), ROWS), pl.ds(aligned(tile, PAIR), PAIR)],
            CONTEXT + 3 * tile + slot,
            device,
        )

    def context_copies(tile):
        return (
            context_copy(tile, 0, x_next, to_xr),
            context_copy(tile, 1, x_prev, to_xl),
            context_copy(tile, 2, x_far, to_xf),
        )

    def rotated(u, gain, cos, sin):
        normal = u * lax.rsqrt(head_mean(u * u) + EPSILON) * gain
        return normal * cos + half_turn(normal) * sin

    def project(block):
        rows = pl.ds(aligned(block, ROWS), ROWS)

        def pair(tile, carry):
            out = dot(span[block], weights[:, pl.ds(aligned(tile, PAIR), PAIR)])
            for side in range(2):
                u = out[:, side * HEAD : (side + 1) * HEAD]
                head = 2 * tile + side
                u_query[head, rows, :] = u
                turned = rotated(u, q_gain[...], cosine[rows, :], sine[rows, :])
                queries[head, rows, :] = turned.astype(BF16)
                queries_t[head, :, rows] = turned.T.astype(BF16)
            return carry

        lax.fori_loop(0, HEADS // 2, pair, 0)
        out = dot(span[block], weights[:, QUERY_COLUMNS:])
        u = out[:, :HEAD]
        u_key[rows, :] = u
        keys[rows, :] = rotated(u, k_gain[...], cosine[rows, :], sine[rows, :]).astype(BF16)
        values[rows, :] = out[:, HEAD:].astype(BF16)

    def transpose_rows(block):
        def chunk(i, carry):
            features = pl.ds(aligned(i, 256), 256)
            columns = pl.ds(aligned(block, ROWS), ROWS)
            span_t[features, columns] = span[block, :, features].astype(F32).T.astype(BF16)
            return carry

        lax.fori_loop(0, FEATURES // 256, chunk, 0)

    own_rows.wait()
    for copy in own_weights:
        copy.wait()
    project(x)
    right_low.wait_recv()
    left_high.wait_recv()
    pass_right.start()
    pass_left.start()

    def send_context(tile, carry):
        for copy in context_copies(tile):
            copy.start()
        return carry

    lax.fori_loop(0, TILES - 1, send_context, 0)
    transpose_rows(x)
    right_high.wait_recv()
    project(x_prev)
    left_low.wait_recv()
    project(x_next)
    transpose_rows(x_prev)
    transpose_rows(x_next)
    pass_right.wait_recv()
    pass_left.wait_recv()
    project(x_far)
    transpose_rows(x_far)
    own_context.wait()

    length = lengths[0]

    def norm_gradient(u, gain, grad):
        inverse = lax.rsqrt(head_mean(u * u) + EPSILON)
        weighted = gain * grad
        return inverse * weighted - u * (inverse * inverse * inverse) * head_mean(u * weighted)

    def unrotated(grad, rows):
        return grad * cosine[rows, :] - half_turn(grad) * sine[rows, :]

    def attend(head):
        columns = pl.ds(aligned(head, HEAD), HEAD)
        for first in range(0, SPAN, QUERY_ROWS):
            rows = slice(first, first + QUERY_ROWS)
            seen = first + QUERY_ROWS
            position = lax.broadcasted_iota(jnp.int32, (QUERY_ROWS, 1), 0) + first
            limit = jnp.minimum(position, length - 1)
            key_position = lax.broadcasted_iota(jnp.int32, (QUERY_ROWS, seen), 1)
            key, value = keys[:seen, :], values[:seen, :]
            scores = dot_t(queries[head, rows, :], key)
            weight = jnp.where(key_position <= limit, jnp.exp2(scores * SCORE_SCALE), 0.0)
            probs = weight * (1.0 / jnp.sum(weight, -1, keepdims=True))
            probs_low = probs.astype(BF16)
            context = dot(probs_low, value)
            d_out = jnp.where(position < length, ctx[rows, columns].astype(F32), 0.0)
            d_low = d_out.astype(BF16)
            delta = jnp.sum(d_out * context, -1, keepdims=True)
            d_score = (probs * (dot_t(d_low, value) - delta)).astype(BF16)
            d_query = dot(d_score, key) * SCALE
            grads[rows, columns] = norm_gradient(
                u_query[head, rows, :], q_gain[...], unrotated(d_query, rows)
            ).astype(BF16)
            dk_t[:, :seen] += dot(queries_t[head, :, rows], d_score)
            dv_t[:, :seen] += dot(d_out.T.astype(BF16), probs_low)

    dk_t[...] = jnp.zeros_like(dk_t)
    dv_t[...] = jnp.zeros_like(dv_t)

    def attend_pair(tile):
        for copy in context_copies(tile):
            copy.wait_recv()
        for side in range(2):
            attend(2 * tile + side)

    def key_value_gradients():
        d_key = dk_t[...].T * SCALE
        grads[:, QUERY_COLUMNS : QUERY_COLUMNS + HEAD] = norm_gradient(
            u_key[...], k_gain[...], unrotated(d_key, slice(0, SPAN))
        ).astype(BF16)
        grads[:, QUERY_COLUMNS + HEAD :] = dv_t[...].T.astype(BF16)

    def input_part(block, store):
        def chunk(i, carry):
            features = pl.ds(aligned(i, 256), 256)
            rows = grads[pl.ds(aligned(block, ROWS), ROWS), :]
            store(features, dot_t(rows, weights[features, :]))
            return carry

        lax.fori_loop(0, FEATURES // 256, chunk, 0)

    half = ROWS // 2
    input_copies = [
        remote(dx_far.at[low, :], x_far_r, INPUT, to_xr),
        remote(dx_far.at[high, :], x_far_l, INPUT + 1, to_xl),
        remote(dx_send_r.at[high, :], x_near_r.at[high, :], INPUT + 2, to_xr),
        remote(dx_send_l.at[low, :], x_near_l.at[low, :], INPUT + 3, to_xl),
        remote(dx_send_r.at[low, :], x_near_r.at[low, :], INPUT + 4, to_xr),
        remote(dx_send_l.at[high, :], x_near_l.at[high, :], INPUT + 5, to_xl),
    ]

    def input_first():
        def store_far(features, out):
            dx_far[:, features] = out.astype(BF16)

        def store_next(features, out):
            dx_wait_r[:, features] = out[:half]
            dx_send_r[half:, features] = out[half:].astype(BF16)

        def store_prev(features, out):
            dx_wait_l[:, features] = out[half:]
            dx_send_l[:half, features] = out[:half].astype(BF16)

        input_part(x_far, store_far)
        input_copies[0].start()
        input_copies[1].start()
        input_part(x_next, store_next)
        input_copies[2].start()
        input_part(x_prev, store_prev)
        input_copies[3].start()

    def input_own():
        def store_own(features, out):
            dx_own[:, features] = out

        input_part(x, store_own)

    def input_second():
        def chunk(i, carry):
            features = pl.ds(aligned(i, 256), 256)
            dx_send_r[:half, features] = (
                dx_wait_r[:, features] + x_far_r[:, features].astype(F32)
            ).astype(BF16)
            dx_send_l[half:, features] = (
                dx_wait_l[:, features] + x_far_l[:, features].astype(F32)
            ).astype(BF16)
            return carry

        input_copies[0].wait_recv()
        input_copies[1].wait_recv()
        lax.fori_loop(0, FEATURES // 256, chunk, 0)
        input_copies[4].start()
        input_copies[5].start()

    def input_last():
        def chunk(i, carry):
            features = pl.ds(aligned(i, 256), 256)
            dx_out[:, features] = (
                dx_own[:, features]
                + x_near_r[:, features].astype(F32)
                + x_near_l[:, features].astype(F32)
            ).astype(BF16)
            return carry

        for copy in input_copies[2:]:
            copy.wait_recv()
        lax.fori_loop(0, FEATURES // 256, chunk, 0)

    def core_copy(tile):
        return remote(part_send.at[tile], part_recv.at[tile], CORE + tile, to_core)

    chunk_blocks = 4

    def weight_gradient(tile):
        columns = pl.ds(aligned(tile, PAIR), PAIR)

        def chunk(i, carry):
            features = pl.ds(aligned(i, chunk_blocks * BLOCK_ROWS), chunk_blocks * BLOCK_ROWS)
            out = dot(span_t[features, :], grads[:, columns])
            kept = jnp.where(core == 0, out[:, :HEAD], out[:, HEAD:])
            sent = jnp.where(core == 0, out[:, HEAD:], out[:, :HEAD])
            blocks = pl.ds(i * chunk_blocks, chunk_blocks)
            shape = (chunk_blocks, BLOCK_ROWS, HEAD)
            part[tile, blocks] = kept.astype(BF16).reshape(shape)
            part_send[tile, blocks] = sent.astype(BF16).reshape(shape)
            return carry

        lax.fori_loop(0, BLOCKS // chunk_blocks, chunk, 0)
        core_copy(tile).start()

    half_z = RING_Z // 2

    def y_copies(tile):
        slot = Y_SLOT + 6 * tile

        def blocks(y_at, half_at):
            return part.at[tile, pl.ds(y_at * RING_Z + half_at * half_z, half_z)]

        first, second = pl.ds(0, half_z), pl.ds(half_z, half_z)
        return [
            remote(blocks(y_far, 0), y_far_r.at[tile], slot, to_yr),
            remote(blocks(y_far, 1), y_far_l.at[tile], slot + 1, to_yl),
            remote(blocks(y_next, 1), y_near_r.at[tile, second], slot + 2, to_yr),
            remote(blocks(y_prev, 0), y_near_l.at[tile, first], slot + 3, to_yl),
            remote(blocks(y_next, 0), y_near_r.at[tile, first], slot + 4, to_yr),
            remote(blocks(y_prev, 1), y_near_l.at[tile, second], slot + 5, to_yl),
        ]

    def y_first(tile):
        core_copy(tile).wait_recv()

        def add(i, carry):
            blocks = pl.ds(i * chunk_blocks, chunk_blocks)
            total = part[tile, blocks].astype(F32) + part_recv[tile, blocks].astype(F32)
            part[tile, blocks] = total.astype(BF16)
            return carry

        lax.fori_loop(0, BLOCKS // chunk_blocks, add, 0)
        for copy in y_copies(tile)[:4]:
            copy.start()

    def y_second(tile):
        copies = y_copies(tile)
        copies[0].wait_recv()
        copies[1].wait_recv()
        right = pl.ds(y_next * RING_Z, half_z)
        left = pl.ds(y_prev * RING_Z + half_z, half_z)
        part[tile, right] = (part[tile, right].astype(F32) + y_far_r[tile].astype(F32)).astype(BF16)
        part[tile, left] = (part[tile, left].astype(F32) + y_far_l[tile].astype(F32)).astype(BF16)
        copies[4].start()
        copies[5].start()

    def z_copy_right(tile, step):
        return remote(
            z_send_r.at[tile, step], z_recv_r.at[tile, step], Z_SLOT + 7 * tile + step, to_zr
        )

    def z_copy_left(tile, step):
        return remote(
            z_send_l.at[tile, step], z_recv_l.at[tile, step], Z_SLOT + 7 * tile + 4 + step, to_zl
        )

    def z_step(tile, step):
        ahead = z_total[tile, lax.rem(z + 4 - step, RING_Z)]
        if step > 0:
            z_copy_right(tile, step - 1).wait_recv()
            ahead = ahead + z_recv_r[tile, step - 1].astype(F32)
        z_send_r[tile, step] = ahead.astype(BF16)
        z_copy_right(tile, step).start()
        if step < 3:
            behind = z_total[tile, lax.rem(z + RING_Z - 3 + step, RING_Z)]
            if step > 0:
                z_copy_left(tile, step - 1).wait_recv()
                behind = behind + z_recv_l[tile, step - 1].astype(F32)
            z_send_l[tile, step] = behind.astype(BF16)
            z_copy_left(tile, step).start()

    def z_first(tile):
        for copy in y_copies(tile)[2:]:
            copy.wait_recv()

        def add(i, carry):
            z_total[tile, i] = (
                part[tile, y * RING_Z + i].astype(F32)
                + y_near_r[tile, i].astype(F32)
                + y_near_l[tile, i].astype(F32)
            )
            return carry

        lax.fori_loop(0, RING_Z, add, 0)
        z_step(tile, 0)

    def z_last(tile):
        z_copy_right(tile, 3).wait_recv()
        z_copy_left(tile, 2).wait_recv()
        total = (
            z_total[tile, z]
            + z_recv_r[tile, 3].astype(F32)
            + z_recv_l[tile, 2].astype(F32)
        )
        result[0, tile] = total[:SHARE]
        result[1, tile] = total[SHARE:]

    stages = [
        y_first,
        y_second,
        z_first,
        lambda tile: z_step(tile, 1),
        lambda tile: z_step(tile, 2),
        lambda tile: z_step(tile, 3),
        z_last,
    ]

    def step(turn, carry):
        @pl.when(turn < TILES - 1)
        def _():
            attend_pair(turn)

        @pl.when(turn == TILES - 1)
        def _():
            key_value_gradients()
            input_first()

        @pl.when(turn < TILES)
        def _():
            weight_gradient(turn)

        for late, stage in enumerate(stages, 1):

            @pl.when((turn >= late) & (turn < late + TILES))
            def _(late=late, stage=stage):
                stage(turn - late)

        @pl.when(turn == TILES)
        def _():
            input_own()

        @pl.when(turn == TILES + 2)
        def _():
            input_second()

        return carry

    lax.fori_loop(0, TILES + len(stages), step, 0)

    final = remote(result.at[1 - core], result_recv, FINAL, to_core)
    final.start()
    input_last()
    final.wait_recv()

    mine, other = aligned(core, HEAD), aligned(1 - core, HEAD)
    for tile in range(TILES - 1):
        gq_out[:, pl.ds(tile * PAIR + mine, HEAD)] = result[core, tile]
        gq_out[:, pl.ds(tile * PAIR + other, HEAD)] = result_recv[tile]
    kept, received = result[core, TILES - 1], result_recv[TILES - 1]
    gk_out[...] = jnp.where(core == 0, kept, received)
    gv_out[...] = jnp.where(core == 0, received, kept)

    for copy in (right_low, right_high, left_high, left_low, pass_right, pass_left, final):
        copy.wait_send()
    for copy in input_copies:
        copy.wait_send()

    def drain_context(tile, carry):
        for copy in context_copies(tile):
            copy.wait_send()
        return carry

    def drain(tile, carry):
        core_copy(tile).wait_send()
        for copy in y_copies(tile):
            copy.wait_send()
        for index in range(4):
            z_copy_right(tile, index).wait_send()
        for index in range(3):
            z_copy_left(tile, index).wait_send()
        return carry

    lax.fori_loop(0, TILES - 1, drain_context, 0)
    lax.fori_loop(0, TILES, drain, 0)


def local(normed, w_query, key_weight, value_weight, q_gain, key_norm_gain, ctx_grad, lengths):
    cosine, sine = angle_tables()
    block = (BLOCK_ROWS, HEAD)
    vmem = pl.BlockSpec(memory_space=pltpu.VMEM)
    anywhere = pl.BlockSpec(memory_space=pl.ANY)
    smem = pl.BlockSpec(memory_space=pltpu.SMEM)
    scratch = [
        pltpu.VMEM((FEATURES, COLUMNS), BF16),
        pltpu.VMEM((RING_X, ROWS, FEATURES), BF16),
        pltpu.VMEM((FEATURES, SPAN), BF16),
        pltpu.VMEM((SPAN, QUERY_COLUMNS), BF16),
        pltpu.VMEM((HEADS, SPAN, HEAD), F32),
        pltpu.VMEM((SPAN, HEAD), F32),
        pltpu.VMEM((HEADS, SPAN, HEAD), BF16),
        pltpu.VMEM((HEADS, HEAD, SPAN), BF16),
        pltpu.VMEM((SPAN, HEAD), BF16),
        pltpu.VMEM((SPAN, HEAD), BF16),
        pltpu.VMEM((SPAN, COLUMNS), BF16),
        pltpu.VMEM((HEAD, SPAN), F32),
        pltpu.VMEM((HEAD, SPAN), F32),
        pltpu.VMEM((TILES, BLOCKS) + block, BF16),
        pltpu.VMEM((TILES, BLOCKS) + block, BF16),
        pltpu.VMEM((TILES, BLOCKS) + block, BF16),
        pltpu.VMEM((TILES, RING_Z // 2) + block, BF16),
        pltpu.VMEM((TILES, RING_Z // 2) + block, BF16),
        pltpu.VMEM((TILES, RING_Z) + block, BF16),
        pltpu.VMEM((TILES, RING_Z) + block, BF16),
        pltpu.VMEM((TILES, RING_Z) + block, F32),
        pltpu.VMEM((TILES, 4) + block, BF16),
        pltpu.VMEM((TILES, 3) + block, BF16),
        pltpu.VMEM((TILES, 4) + block, BF16),
        pltpu.VMEM((TILES, 3) + block, BF16),
        pltpu.VMEM((2, TILES, SHARE, HEAD), F32),
        pltpu.VMEM((TILES, SHARE, HEAD), F32),
        pltpu.VMEM((ROWS, FEATURES), BF16),
        pltpu.VMEM((ROWS, FEATURES), BF16),
        pltpu.VMEM((ROWS, FEATURES), BF16),
        pltpu.VMEM((ROWS // 2, FEATURES), F32),
        pltpu.VMEM((ROWS // 2, FEATURES), F32),
        pltpu.VMEM((ROWS, FEATURES), F32),
        pltpu.VMEM((ROWS // 2, FEATURES), BF16),
        pltpu.VMEM((ROWS // 2, FEATURES), BF16),
        pltpu.VMEM((ROWS, FEATURES), BF16),
        pltpu.VMEM((ROWS, FEATURES), BF16),
        pltpu.SemaphoreType.DMA((5,)),
        pltpu.SemaphoreType.DMA((SLOTS,)),
        pltpu.SemaphoreType.DMA((SLOTS,)),
    ]
    return pl.pallas_call(
        kernel,
        out_shape=(
            jax.ShapeDtypeStruct((ROWS, FEATURES), BF16),
            jax.ShapeDtypeStruct((SHARE, QUERY_COLUMNS), F32),
            jax.ShapeDtypeStruct((SHARE, HEAD), F32),
            jax.ShapeDtypeStruct((SHARE, HEAD), F32),
        ),
        in_specs=[anywhere] * 4 + [vmem] * 2 + [anywhere, smem] + [vmem] * 2,
        out_specs=(vmem,) * 4,
        scratch_shapes=scratch,
        compiler_params=pltpu.CompilerParams(
            collective_id=0, has_side_effects=True, vmem_limit_bytes=60 * 2**20
        ),
    )(
        normed,
        w_query,
        key_weight,
        value_weight,
        q_gain.reshape(1, HEAD),
        key_norm_gain.reshape(1, HEAD),
        ctx_grad,
        lengths,
        cosine,
        sine,
    )


def solution(mesh):
    in_specs = (
        P(("dp", "sp"), None),
        P(None, "sp"),
        P(None, "sp"),
        P(None, "sp"),
        P(),
        P(),
        P(("dp", "sp"), None),
        P("dp"),
    )
    out_specs = (P(("dp", "sp"), None), P("dp", "sp"), P("dp", "sp"), P("dp", "sp"))
    return jax.shard_map(local, mesh=mesh, in_specs=in_specs, out_specs=out_specs, check_vma=False)
```

time: 356 us -> 113 us (0.32); the launches traced: 352 us -> 113 us
  waiting for transfers between devices: 228 us -> 0 us
  Pallas kernels: 0 us -> 105 us
  matrix products: 51.6 us -> 0 us
  local copies, waits for them, and re-layouts: 40.3 us -> 6.23 us
  between operations: 15.3 us -> 1.29 us
  other arithmetic: 11.1 us -> 0 us
  starting transfers between devices: 4.92 us -> 0 us
    unnamed x4 -> x0, waiting for transfers between devices: 160 us -> none
    pallas_call x0 -> x1, Pallas kernels: none -> 105 us  [local(): pl.pallas_call(kernel, out_shape=(jax.ShapeDtypeStruct((ROWS, FEATURES),...]
    dot_general x55 -> x0, matrix products: 51.6 us -> none  [the longest x8 10.3 us: local(): lax.dot_general(q_head, k_head, (((1,), (1,)), ((), ())), preferred_eleme...]
    reduce_scatter x1 -> x0, waiting for transfers between devices: 34.4 us -> none  [local(): lax.psum_scatter(total + lax.dot_general(value_gradient, value_weight, ((...]
    unnamed x79 -> x4, local copies, waits for them, and re-layouts: 29 us -> 6.23 us
    all_gather x1 -> x0, waiting for transfers between devices: 21.5 us -> none  [local(): span = lax.all_gather(normed, 'sp', axis=0, tiled=True)]
    all_to_all x1 -> x0, waiting for transfers between devices: 12 us -> none  [local(): lax.all_to_all(ctx_grad, 'sp', split_axis=1, concat_axis=0, tiled=True)]
    slice x4 -> x0, local copies, waits for them, and re-layouts: 5.48 us -> none  [the longest x1 2.52 us: local(): q_proj[:, head_index]]
  transfers between devices with their start and end apart: 4 -> 0, of which waited for: 4 -> 0; matrix products, arithmetic and copies ran while one was open for 9% -> 0% of each run, Pallas kernels for 0% -> 0%
where the time goes in v1:
time: 113 us
  Pallas kernels  105 us (93%)
  local copies, waits for them, and re-layouts  6.23 us (6%)
  between operations  1.29 us (1%)
    pallas_call x1, Pallas kernels, local(): pl.pallas_call(kernel, out_shape=(jax.ShapeDtypeStruct((ROWS, FEATURES),...  105 us
    unnamed x4, local copies, waits for them, and re-layouts  6.23 us

profile of v1, /device:TPU:1, one launch (start us, length us, event | category | flops | bytes accessed | tf_op | source)
XLA Modules:
  0.0 112.7 jit_solution(17049725815807110501)
XLA Ops:
  1.3 105.2 %shard_map.129 = (bf16[128,2560]{1,0:T(8,128)(2,1)}, f32[40,1024]{1,0:T(8,128)}, f32[40,128]{1,0:T(8,128)}, f32[40,128]{1,0:T(8,128)}) custom-call(bf16[128,2560]{1,0:T(8,128)(2,1)} %normed.1, bf16[2560,1024]{1,0:T(8,128)(2,1)} %w_query.1, bf16[2560,128]{1,0:T(8,128)(2,1)} %key_weight.1, bf16[2560,128]{1,0:T(8,128)(2,1)} %value_weight.1, f32[1,128]{1,0:T(1,128)} %bitcast.2, ...), custom_call_target="tpu_custom_call" | custom-call | tf_op jit(solution)/shard_map/pallas_call | solution.py:602
  106.5 2.0 %copy.19 = bf16[128,2560]{1,0:T(8,128)(2,1)} copy(bf16[128,2560]{1,0:T(8,128)(2,1)} %get-tuple-element.8) | data formatting | bytes 1310720
  108.5 1.6 %copy.20 = f32[40,1024]{1,0:T(8,128)} copy(f32[40,1024]{1,0:T(8,128)} %get-tuple-element.9) | data formatting | bytes 327680
  110.1 1.3 %copy.21 = f32[40,128]{1,0:T(8,128)} copy(f32[40,128]{1,0:T(8,128)} %get-tuple-element.10) | data formatting | bytes 40960
  111.4 1.3 %copy.22 = f32[40,128]{1,0:T(8,128)} copy(f32[40,128]{1,0:T(8,128)} %get-tuple-element.11) | data formatting | bytes 40960

commit v2 on v1

v2 whole, which is shorter than its diff:
```python
import math

import jax
import jax.numpy as jnp
import numpy as np
from jax import lax
from jax.experimental import pallas as pl
from jax.experimental.pallas import tpu as pltpu
from jax.sharding import PartitionSpec as P

F32 = jnp.float32
BF16 = jnp.bfloat16
EPSILON = 1e-06
LOG_BASE = math.log(1000000.0)
RING_X, RING_Y, RING_Z = 4, 4, 8
ROWS = 128
SPAN = 512
FEATURES = 2560
HEADS = 8
HEAD = 128
QUERY_COLUMNS = HEADS * HEAD
COLUMNS = QUERY_COLUMNS + 2 * HEAD
PAIR = 2 * HEAD
TILES = COLUMNS // PAIR
BLOCKS = RING_Y * RING_Z
BLOCK_ROWS = FEATURES // BLOCKS
SHARE = BLOCK_ROWS // 2
SCALE = HEAD**-0.5
SCORE_SCALE = SCALE * math.log2(math.e)
QUERY_ROWS = 256
RINGED = (0, 2)
STRAIGHT = (1, 3, 4)

GATHER = 0
CONTEXT = GATHER + 6
CORE = CONTEXT + 3 * (TILES - 1)
RING_SLOT = CORE + TILES
FINAL = RING_SLOT + 10 * TILES
INPUT = FINAL + 1
SLOTS = INPUT + 10


def angle_tables():
    position = np.arange(SPAN, dtype=np.float32)
    freqs = np.exp(np.arange(HEAD // 2, dtype=np.float32) * np.float32(-2.0 * LOG_BASE / HEAD))
    angles = position[:, None] * freqs.astype(np.float32)[None, :]
    cosine, sine = np.cos(angles), np.sin(angles)
    return (
        np.concatenate([cosine, cosine], 1).astype(np.float32),
        np.concatenate([-sine, sine], 1).astype(np.float32),
    )


def dot(a, b):
    return jnp.dot(a, b, preferred_element_type=F32)


def dot_t(a, b):
    return lax.dot_general(a, b, (((1,), (1,)), ((), ())), preferred_element_type=F32)


def half_turn(a):
    return pltpu.roll(a, HEAD // 2, 1)


def head_mean(a):
    return jnp.sum(a, -1, keepdims=True) * (1.0 / HEAD)


def aligned(index, unit):
    return pl.multiple_of(index * unit, unit)


def kernel(
    normed, w_query, key_weight, value_weight, q_gain, k_gain, ctx_in, lengths, cosine_in, sine_in,
    dx_out, gq_out, gk_out, gv_out,
    cosine, sine, weights, weights_t, span, span_t, ctx, u_query, u_key, queries, queries_t, keys, values,
    grads, dk_t, dv_t,
    part, part_send, part_recv, y_recv, z_send, z_recv,
    long_send, long_recv, short_send, short_recv, last_send, last_recv,
    own_total, result, result_recv,
    dx_far, dx_send_r, dx_send_l, dx_wait_r, dx_wait_l, dx_own,
    x_far_r, x_far_l, x_near_r, x_near_l,
    local_sem, send_sem, recv_sem,
):
    dp = lax.axis_index("dp")
    x = lax.axis_index("sp")
    core = lax.rem(dp, 2)
    z = lax.rem(lax.div(dp, 2), RING_Z)
    y = lax.div(dp, 2 * RING_Z)

    def place(y_at, z_at, core_at):
        return (y_at * RING_Z + z_at) * 2 + core_at

    x_next, x_prev, x_far = lax.rem(x + 1, RING_X), lax.rem(x + 3, RING_X), lax.rem(x + 2, RING_X)
    to_xr, to_xl, to_xf = (dp, x_next), (dp, x_prev), (dp, x_far)
    to_core = (place(y, z, 1 - core), x)
    partners = [to_xr, to_xl, to_xf, to_core]
    partners += [(place(lax.rem(y + k, RING_Y), z, core), x) for k in range(1, RING_Y)]
    partners += [(place(y, lax.rem(z + k, RING_Z), core), x) for k in range(1, RING_Z)]

    def remote(src, dst, slot, device):
        return pltpu.make_async_remote_copy(
            src_ref=src,
            dst_ref=dst,
            send_sem=send_sem.at[slot],
            recv_sem=recv_sem.at[slot],
            device_id=device,
            device_id_type=pl.DeviceIdType.MESH,
        )

    own_rows = pltpu.make_async_copy(normed, span.at[x], local_sem.at[0])
    own_weights = [
        pltpu.make_async_copy(w_query, weights.at[:, pl.ds(0, QUERY_COLUMNS)], local_sem.at[1]),
        pltpu.make_async_copy(
            key_weight, weights.at[:, pl.ds(QUERY_COLUMNS, HEAD)], local_sem.at[2]
        ),
        pltpu.make_async_copy(
            value_weight, weights.at[:, pl.ds(QUERY_COLUMNS + HEAD, HEAD)], local_sem.at[3]
        ),
    ]
    own_context = pltpu.make_async_copy(
        ctx_in.at[:, pl.ds(aligned(x, QUERY_COLUMNS), QUERY_COLUMNS)],
        ctx.at[pl.ds(aligned(x, ROWS), ROWS), :],
        local_sem.at[4],
    )
    tables = [
        pltpu.make_async_copy(cosine_in, cosine, local_sem.at[5]),
        pltpu.make_async_copy(sine_in, sine, local_sem.at[6]),
    ]
    own_rows.start()
    for copy in own_weights + tables:
        copy.start()
    own_context.start()

    barrier = pltpu.get_barrier_semaphore()
    for device in partners:
        pl.semaphore_signal(barrier, inc=1, device_id=device, device_id_type=pl.DeviceIdType.MESH)
    pl.semaphore_wait(barrier, len(partners))

    low, high = pl.ds(0, ROWS // 2), pl.ds(ROWS // 2, ROWS // 2)

    def gather_own(slot, half, device):
        return remote(normed.at[half, :], span.at[x, half, :], GATHER + slot, device)

    def gather_pass(slot, owner, half, device):
        return remote(
            span.at[owner, half, :], span.at[owner, half, :], GATHER + slot, device
        )

    right_low, right_high = gather_own(0, low, to_xr), gather_own(1, high, to_xr)
    left_high, left_low = gather_own(2, high, to_xl), gather_own(3, low, to_xl)
    pass_right = gather_pass(4, x_prev, low, to_xr)
    pass_left = gather_pass(5, x_next, high, to_xl)
    right_low.start()
    left_high.start()
    right_high.start()
    left_low.start()

    def context_copy(tile, slot, owner, device):
        start = pl.multiple_of(owner * QUERY_COLUMNS + tile * PAIR, PAIR)
        return remote(
            ctx_in.at[:, pl.ds(start, PAIR)],
            ctx.at[pl.ds(aligned(x, ROWS), ROWS), pl.ds(aligned(tile, PAIR), PAIR)],
            CONTEXT + 3 * tile + slot,
            device,
        )

    def context_copies(tile):
        return (
            context_copy(tile, 0, x_next, to_xr),
            context_copy(tile, 1, x_prev, to_xl),
            context_copy(tile, 2, x_far, to_xf),
        )

    def rotated(u, gain, cos, sin):
        normal = u * lax.rsqrt(head_mean(u * u) + EPSILON) * gain
        return normal * cos + half_turn(normal) * sin

    def project(block):
        rows = pl.ds(aligned(block, ROWS), ROWS)

        def pair(tile, carry):
            out = dot(span[block], weights[:, pl.ds(aligned(tile, PAIR), PAIR)])
            for side in range(2):
                u = out[:, side * HEAD : (side + 1) * HEAD]
                head = 2 * tile + side
                u_query[head, rows, :] = u
                turned = rotated(u, q_gain[...], cosine[rows, :], sine[rows, :])
                queries[head, rows, :] = turned.astype(BF16)
                queries_t[head, :, rows] = turned.T.astype(BF16)
            return carry

        lax.fori_loop(0, HEADS // 2, pair, 0)
        out = dot(span[block], weights[:, QUERY_COLUMNS:])
        u = out[:, :HEAD]
        u_key[rows, :] = u
        keys[rows, :] = rotated(u, k_gain[...], cosine[rows, :], sine[rows, :]).astype(BF16)
        values[rows, :] = out[:, HEAD:].astype(BF16)

    def rotated_rows(block):
        return pl.ds(aligned(lax.rem(block - x + 1 + RING_X, RING_X), ROWS), ROWS)

    def transpose_rows(block):
        def chunk(i, carry):
            features = pl.ds(aligned(i, 256), 256)
            span_t[features, rotated_rows(block)] = span[block, :, features].T
            return carry

        lax.fori_loop(0, FEATURES // 256, chunk, 0)

    def transpose_weights():
        def chunk(i, carry):
            features = pl.ds(aligned(i, 256), 256)
            for first in range(0, COLUMNS, PAIR):
                columns = slice(first, first + PAIR)
                weights_t[columns, features] = weights[features, columns].T
            return carry

        lax.fori_loop(0, FEATURES // 256, chunk, 0)

    own_rows.wait()
    for copy in own_weights + tables:
        copy.wait()
    project(x)
    right_low.wait_recv()
    left_high.wait_recv()
    pass_right.start()
    pass_left.start()

    def send_context(tile, carry):
        for copy in context_copies(tile):
            copy.start()
        return carry

    lax.fori_loop(0, TILES - 1, send_context, 0)
    transpose_rows(x)
    transpose_weights()
    right_high.wait_recv()
    project(x_prev)
    left_low.wait_recv()
    project(x_next)
    transpose_rows(x_prev)
    transpose_rows(x_next)
    pass_right.wait_recv()
    pass_left.wait_recv()
    project(x_far)
    transpose_rows(x_far)
    own_context.wait()

    length = lengths[0]

    def norm_gradient(u, gain, grad):
        inverse = lax.rsqrt(head_mean(u * u) + EPSILON)
        weighted = gain * grad
        return inverse * weighted - u * (inverse * inverse * inverse) * head_mean(u * weighted)

    def unrotated(grad, rows):
        return grad * cosine[rows, :] - half_turn(grad) * sine[rows, :]

    def store_grads(first, columns, values):
        low_values = values.astype(BF16)
        for start in range(0, values.shape[0], ROWS):
            target = rotated_rows((first + start) // ROWS)
            grads[target, columns] = low_values[start : start + ROWS]

    def attend(head):
        columns = pl.ds(aligned(head, HEAD), HEAD)
        for first in range(0, SPAN, QUERY_ROWS):
            rows = slice(first, first + QUERY_ROWS)
            seen = first + QUERY_ROWS
            position = lax.broadcasted_iota(jnp.int32, (QUERY_ROWS, 1), 0) + first
            limit = jnp.minimum(position, length - 1)
            key_position = lax.broadcasted_iota(jnp.int32, (QUERY_ROWS, seen), 1)
            key, value = keys[:seen, :], values[:seen, :]
            scores = dot_t(queries[head, rows, :], key)
            weight = jnp.where(key_position <= limit, jnp.exp2(scores * SCORE_SCALE), 0.0)
            probs = weight * (1.0 / jnp.sum(weight, -1, keepdims=True))
            probs_low = probs.astype(BF16)
            context = dot(probs_low, value)
            d_out = jnp.where(position < length, ctx[rows, columns].astype(F32), 0.0)
            d_low = d_out.astype(BF16)
            delta = jnp.sum(d_out * context, -1, keepdims=True)
            d_score = (probs * (dot_t(d_low, value) - delta)).astype(BF16)
            d_query = dot(d_score, key) * SCALE
            store_grads(
                first,
                columns,
                norm_gradient(u_query[head, rows, :], q_gain[...], unrotated(d_query, rows)),
            )
            dk_t[:, :seen] += dot(queries_t[head, :, rows], d_score)
            dv_t[:, :seen] += dot(d_out.T.astype(BF16), probs_low)

    dk_t[...] = jnp.zeros_like(dk_t)
    dv_t[...] = jnp.zeros_like(dv_t)

    def attend_pair(tile):
        for copy in context_copies(tile):
            copy.wait_recv()
        for side in range(2):
            attend(2 * tile + side)

    def key_value_gradients():
        d_key = dk_t[...].T * SCALE
        store_grads(
            0,
            slice(QUERY_COLUMNS, QUERY_COLUMNS + HEAD),
            norm_gradient(u_key[...], k_gain[...], unrotated(d_key, slice(0, SPAN))),
        )
        store_grads(0, slice(QUERY_COLUMNS + HEAD, COLUMNS), dv_t[...].T)

    half = ROWS // 2
    sides = [pl.ds(0, FEATURES // 2), pl.ds(FEATURES // 2, FEATURES // 2)]
    far_copies, near_copies = [], []
    for i, side in enumerate(sides):
        far_copies += [
            remote(dx_far.at[low, side], x_far_r.at[:, side], INPUT + 4 * i, to_xr),
            remote(dx_far.at[high, side], x_far_l.at[:, side], INPUT + 4 * i + 1, to_xl),
        ]
        near_copies += [
            remote(dx_send_r.at[low, side], x_near_r.at[low, side], INPUT + 4 * i + 2, to_xr),
            remote(dx_send_l.at[high, side], x_near_l.at[high, side], INPUT + 4 * i + 3, to_xl),
        ]
    first_copies = [
        remote(dx_send_r.at[high, :], x_near_r.at[high, :], INPUT + 8, to_xr),
        remote(dx_send_l.at[low, :], x_near_l.at[low, :], INPUT + 9, to_xl),
    ]
    chunks = FEATURES // 512

    def input_first(side):
        def chunk(i, carry):
            features = pl.ds(aligned(i, 256), 256)
            out = dot(grads[...], weights_t[:, features])
            dx_far[:, features] = out[3 * ROWS :].astype(BF16)
            dx_wait_l[:, features] = out[half:ROWS]
            dx_send_l[:half, features] = out[:half].astype(BF16)
            dx_own[:, features] = out[ROWS : 2 * ROWS]
            dx_wait_r[:, features] = out[2 * ROWS : 2 * ROWS + half]
            dx_send_r[half:, features] = out[2 * ROWS + half : 3 * ROWS].astype(BF16)
            return carry

        lax.fori_loop(side * chunks, (side + 1) * chunks, chunk, 0)
        for copy in far_copies[2 * side : 2 * side + 2]:
            copy.start()
        if side == 1:
            for copy in first_copies:
                copy.start()

    def input_second(side):
        def chunk(i, carry):
            features = pl.ds(aligned(i, 256), 256)
            dx_send_r[:half, features] = (
                dx_wait_r[:, features] + x_far_r[:, features].astype(F32)
            ).astype(BF16)
            dx_send_l[half:, features] = (
                dx_wait_l[:, features] + x_far_l[:, features].astype(F32)
            ).astype(BF16)
            return carry

        for copy in far_copies[2 * side : 2 * side + 2]:
            copy.wait_recv()
        lax.fori_loop(side * chunks, (side + 1) * chunks, chunk, 0)
        for copy in near_copies[2 * side : 2 * side + 2]:
            copy.start()

    def input_last():
        def chunk(i, carry):
            features = pl.ds(aligned(i, 256), 256)
            dx_out[:, features] = (
                dx_own[:, features]
                + x_near_r[:, features].astype(F32)
                + x_near_l[:, features].astype(F32)
            ).astype(BF16)
            return carry

        for copy in first_copies + near_copies:
            copy.wait_recv()
        lax.fori_loop(0, FEATURES // 256, chunk, 0)

    def core_copy(tile):
        return remote(part_send.at[tile], part_recv.at[tile], CORE + tile, to_core)

    chunk_blocks = 4

    def weight_gradient(tile):
        columns = pl.ds(aligned(tile, PAIR), PAIR)
        by_z = lax.rem(tile + 1, 2) * (1 - lax.div(tile, 4))

        def chunk(i, carry):
            features = pl.ds(aligned(i, chunk_blocks * BLOCK_ROWS), chunk_blocks * BLOCK_ROWS)
            out = dot(span_t[features, :], grads[:, columns])
            kept = jnp.where(core == 0, out[:, :HEAD], out[:, HEAD:]).astype(BF16)
            sent = jnp.where(core == 0, out[:, HEAD:], out[:, :HEAD]).astype(BF16)
            for j in range(chunk_blocks):
                block = chunk_blocks * i + j
                block_z, block_y = lax.rem(block, RING_Z), lax.div(block, RING_Z)
                at = by_z * (block_z * RING_Y + block_y) + (1 - by_z) * block
                rows = slice(j * BLOCK_ROWS, (j + 1) * BLOCK_ROWS)
                part[tile, at] = kept[rows]
                part_send[tile, at] = sent[rows]
            return carry

        lax.fori_loop(0, BLOCKS // chunk_blocks, chunk, 0)
        core_copy(tile).start()

    def add_cores(tile):
        def add(i, carry):
            blocks = pl.ds(i * chunk_blocks, chunk_blocks)
            total = part[tile, blocks].astype(F32) + part_recv[tile, blocks].astype(F32)
            part[tile, blocks] = total.astype(BF16)
            return carry

        core_copy(tile).wait_recv()
        lax.fori_loop(0, BLOCKS // chunk_blocks, add, 0)

    def store_result(tile, total):
        result[0, tile] = total[:SHARE]
        result[1, tile] = total[SHARE:]

    def y_copies(tile):
        slot = RING_SLOT + 10 * tile
        index = STRAIGHT.index(tile)
        return [
            remote(
                part.at[tile, pl.ds(lax.rem(y + k, RING_Y) * RING_Z, RING_Z)],
                y_recv.at[index, k - 1],
                slot + k - 1,
                (place(lax.rem(y + k, RING_Y), z, core), x),
            )
            for k in (1, 2, 3)
        ]

    def z_copies(tile):
        slot = RING_SLOT + 10 * tile + 3
        index = STRAIGHT.index(tile)
        return [
            remote(
                z_send.at[index, k - 1],
                z_recv.at[index, k - 1],
                slot + k - 1,
                (place(y, lax.rem(z + k, RING_Z), core), x),
            )
            for k in range(1, RING_Z)
        ]

    def straight_first(tile):
        add_cores(tile)
        for copy in y_copies(tile):
            copy.start()

    def straight_second(tile):
        index = STRAIGHT.index(tile)
        for copy in y_copies(tile):
            copy.wait_recv()
        copies = z_copies(tile)
        for k in (1, 2, 3, 4, 5, 6, 7, 0):
            block = lax.rem(z + k, RING_Z)
            total = part[tile, y * RING_Z + block].astype(F32)
            for i in range(3):
                total = total + y_recv[index, i, block].astype(F32)
            if k:
                z_send[index, k - 1] = total.astype(BF16)
                copies[k - 1].start()
            else:
                own_total[tile] = total

    def straight_third(tile):
        index = STRAIGHT.index(tile)
        for copy in z_copies(tile):
            copy.wait_recv()
        total = own_total[tile]
        for i in range(RING_Z - 1):
            total = total + z_recv[index, i].astype(F32)
        store_result(tile, total)

    sign = 1 - 2 * core

    def ahead(k):
        return lax.rem(z + RING_Z + sign * k, RING_Z)

    to_long, to_short = (place(y, ahead(1), core), x), (place(y, ahead(-1), core), x)

    def long_copy(tile, step):
        index = RINGED.index(tile)
        return remote(
            long_send.at[index, step], long_recv.at[index, step], RING_SLOT + 10 * tile + step, to_long
        )

    def short_copy(tile, step):
        index = RINGED.index(tile)
        return remote(
            short_send.at[index, step],
            short_recv.at[index, step],
            RING_SLOT + 10 * tile + 4 + step,
            to_short,
        )

    def ring_part(tile, block):
        return part[tile, pl.ds(block * RING_Y, RING_Y)].astype(F32)

    def ring_step(tile, step):
        index = RINGED.index(tile)
        if step == 0:
            add_cores(tile)
        total = ring_part(tile, ahead(4 - step))
        if step > 0:
            long_copy(tile, step - 1).wait_recv()
            total = total + long_recv[index, step - 1].astype(F32)
        long_send[index, step] = total.astype(BF16)
        long_copy(tile, step).start()
        if step < 3:
            total = ring_part(tile, ahead(step - 3))
            if step > 0:
                short_copy(tile, step - 1).wait_recv()
                total = total + short_recv[index, step - 1].astype(F32)
            short_send[index, step] = total.astype(BF16)
            short_copy(tile, step).start()

    def last_copies(tile):
        index = RINGED.index(tile)
        return [
            remote(
                last_send.at[index, k - 1],
                last_recv.at[index, k - 1],
                RING_SLOT + 10 * tile + 7 + k - 1,
                (place(lax.rem(y + k, RING_Y), z, core), x),
            )
            for k in (1, 2, 3)
        ]

    def ring_fifth(tile):
        index = RINGED.index(tile)
        long_copy(tile, 3).wait_recv()
        short_copy(tile, 2).wait_recv()
        copies = last_copies(tile)
        for k in (1, 2, 3, 0):
            block = lax.rem(y + k, RING_Y)
            total = (
                part[tile, z * RING_Y + block].astype(F32)
                + long_recv[index, 3, block].astype(F32)
                + short_recv[index, 2, block].astype(F32)
            )
            if k:
                last_send[index, k - 1] = total.astype(BF16)
                copies[k - 1].start()
            else:
                own_total[tile] = total

    def ring_sixth(tile):
        index = RINGED.index(tile)
        for copy in last_copies(tile):
            copy.wait_recv()
        total = own_total[tile]
        for i in range(3):
            total = total + last_recv[index, i].astype(F32)
        store_result(tile, total)

    def step(turn, carry):
        attend_pair(turn)

        @pl.when(turn < TILES - 2)
        def _():
            weight_gradient(turn)

        @pl.when(turn == 1)
        def _():
            ring_step(0, 0)

        @pl.when(turn == 2)
        def _():
            straight_first(1)
            ring_step(0, 1)

        return carry

    lax.fori_loop(0, TILES - 1, step, 0)
    key_value_gradients()
    input_first(0)
    weight_gradient(3)
    weight_gradient(4)
    input_first(1)
    ring_step(2, 0)
    ring_step(0, 2)
    straight_first(3)
    straight_first(4)
    straight_second(1)
    ring_step(2, 1)
    ring_step(0, 3)
    input_second(0)
    ring_step(2, 2)
    straight_third(1)
    ring_fifth(0)
    input_second(1)
    ring_step(2, 3)
    straight_second(3)
    ring_sixth(0)
    ring_fifth(2)
    straight_second(4)
    straight_third(3)
    ring_sixth(2)
    straight_third(4)

    final = remote(result.at[1 - core], result_recv, FINAL, to_core)
    final.start()
    input_last()
    final.wait_recv()

    mine, other = aligned(core, HEAD), aligned(1 - core, HEAD)
    for tile in range(TILES - 1):
        gq_out[:, pl.ds(tile * PAIR + mine, HEAD)] = result[core, tile]
        gq_out[:, pl.ds(tile * PAIR + other, HEAD)] = result_recv[tile]
    kept, received = result[core, TILES - 1], result_recv[TILES - 1]
    gk_out[...] = jnp.where(core == 0, kept, received)
    gv_out[...] = jnp.where(core == 0, received, kept)

    for copy in (right_low, right_high, left_high, left_low, pass_right, pass_left, final):
        copy.wait_send()
    for copy in far_copies + near_copies + first_copies:
        copy.wait_send()

    def drain_context(tile, carry):
        for copy in context_copies(tile):
            copy.wait_send()
        return carry

    lax.fori_loop(0, TILES - 1, drain_context, 0)
    for tile in range(TILES):
        copies = [core_copy(tile)]
        if tile in RINGED:
            copies += [long_copy(tile, i) for i in range(4)] + [short_copy(tile, i) for i in range(3)]
            copies += last_copies(tile)
        else:
            copies += y_copies(tile) + z_copies(tile)
        for copy in copies:
            copy.wait_send()


def write_results(*refs):
    for source, target in zip(refs[:4], refs[4:]):
        target[...] = source[...]


def local(normed, w_query, key_weight, value_weight, q_gain, key_norm_gain, ctx_grad, lengths):
    cosine, sine = angle_tables()
    block = (BLOCK_ROWS, HEAD)
    vmem = pl.BlockSpec(memory_space=pltpu.VMEM)
    anywhere = pl.BlockSpec(memory_space=pl.ANY)
    smem = pl.BlockSpec(memory_space=pltpu.SMEM)
    scratch = [
        pltpu.VMEM((SPAN, HEAD), F32),
        pltpu.VMEM((SPAN, HEAD), F32),
        pltpu.VMEM((FEATURES, COLUMNS), BF16),
        pltpu.VMEM((COLUMNS, FEATURES), BF16),
        pltpu.VMEM((RING_X, ROWS, FEATURES), BF16),
        pltpu.VMEM((FEATURES, SPAN), BF16),
        pltpu.VMEM((SPAN, QUERY_COLUMNS), BF16),
        pltpu.VMEM((HEADS, SPAN, HEAD), F32),
        pltpu.VMEM((SPAN, HEAD), F32),
        pltpu.VMEM((HEADS, SPAN, HEAD), BF16),
        pltpu.VMEM((HEADS, HEAD, SPAN), BF16),
        pltpu.VMEM((SPAN, HEAD), BF16),
        pltpu.VMEM((SPAN, HEAD), BF16),
        pltpu.VMEM((SPAN, COLUMNS), BF16),
        pltpu.VMEM((HEAD, SPAN), F32),
        pltpu.VMEM((HEAD, SPAN), F32),
        pltpu.VMEM((TILES, BLOCKS) + block, BF16),
        pltpu.VMEM((TILES, BLOCKS) + block, BF16),
        pltpu.VMEM((TILES, BLOCKS) + block, BF16),
        pltpu.VMEM((len(STRAIGHT), 3, RING_Z) + block, BF16),
        pltpu.VMEM((len(STRAIGHT), RING_Z - 1) + block, BF16),
        pltpu.VMEM((len(STRAIGHT), RING_Z - 1) + block, BF16),
        pltpu.VMEM((len(RINGED), 4, RING_Y) + block, BF16),
        pltpu.VMEM((len(RINGED), 4, RING_Y) + block, BF16),
        pltpu.VMEM((len(RINGED), 3, RING_Y) + block, BF16),
        pltpu.VMEM((len(RINGED), 3, RING_Y) + block, BF16),
        pltpu.VMEM((len(RINGED), 3) + block, BF16),
        pltpu.VMEM((len(RINGED), 3) + block, BF16),
        pltpu.VMEM((TILES,) + block, F32),
        pltpu.VMEM((2, TILES, SHARE, HEAD), F32),
        pltpu.VMEM((TILES, SHARE, HEAD), F32),
        pltpu.VMEM((ROWS, FEATURES), BF16),
        pltpu.VMEM((ROWS, FEATURES), BF16),
        pltpu.VMEM((ROWS, FEATURES), BF16),
        pltpu.VMEM((ROWS // 2, FEATURES), F32),
        pltpu.VMEM((ROWS // 2, FEATURES), F32),
        pltpu.VMEM((ROWS, FEATURES), F32),
        pltpu.VMEM((ROWS // 2, FEATURES), BF16),
        pltpu.VMEM((ROWS // 2, FEATURES), BF16),
        pltpu.VMEM((ROWS, FEATURES), BF16),
        pltpu.VMEM((ROWS, FEATURES), BF16),
        pltpu.SemaphoreType.DMA((7,)),
        pltpu.SemaphoreType.DMA((SLOTS,)),
        pltpu.SemaphoreType.DMA((SLOTS,)),
    ]
    out_shape = (
        jax.ShapeDtypeStruct((ROWS, FEATURES), BF16),
        jax.ShapeDtypeStruct((SHARE, QUERY_COLUMNS), F32),
        jax.ShapeDtypeStruct((SHARE, HEAD), F32),
        jax.ShapeDtypeStruct((SHARE, HEAD), F32),
    )
    results = pl.pallas_call(
        kernel,
        out_shape=out_shape,
        in_specs=[anywhere] * 4 + [vmem] * 2 + [anywhere, smem, anywhere, anywhere],
        out_specs=(vmem,) * 4,
        scratch_shapes=scratch,
        compiler_params=pltpu.CompilerParams(
            collective_id=0, has_side_effects=True, vmem_limit_bytes=60 * 2**20
        ),
    )(
        normed,
        w_query,
        key_weight,
        value_weight,
        q_gain.reshape(1, HEAD),
        key_norm_gain.reshape(1, HEAD),
        ctx_grad,
        lengths,
        cosine,
        sine,
    )
    return pl.pallas_call(
        write_results,
        out_shape=out_shape,
        in_specs=[vmem] * 4,
        out_specs=(vmem,) * 4,
    )(*results)


def solution(mesh):
    in_specs = (
        P(("dp", "sp"), None),
        P(None, "sp"),
        P(None, "sp"),
        P(None, "sp"),
        P(),
        P(),
        P(("dp", "sp"), None),
        P("dp"),
    )
    out_specs = (P(("dp", "sp"), None), P("dp", "sp"), P("dp", "sp"), P("dp", "sp"))
    return jax.shard_map(local, mesh=mesh, in_specs=in_specs, out_specs=out_specs, check_vma=False)
```

time: 113 us -> 99.2 us (0.88)
  Pallas kernels: 105 us -> 97.8 us
  local copies, waits for them, and re-layouts: 6.23 us -> 0 us
    pallas_call x1 -> x2, Pallas kernels: 105 us -> 97.8 us  [the longest x1 95.7 us: local(): pl.pallas_call(kernel, out_shape=out_shape, in_specs=[anywhere] * 4 + [vm...]
    unnamed x4 -> x0, local copies, waits for them, and re-layouts: 6.23 us -> none
where the time goes in v2:
time: 99.2 us; the launch traced here: 99.1 us
  Pallas kernels  97.8 us (99%)
  between operations  1.29 us (1%)
    pallas_call x1, Pallas kernels, local(): pl.pallas_call(kernel, out_shape=out_shape, in_specs=[anywhere] * 4 + [vm...  95.7 us
    pallas_call x1, Pallas kernels, local(): pl.pallas_call(write_results, out_shape=out_shape, in_specs=[vmem] * 4, o...  2.09 us

profile of v2, /device:TPU:1, one launch (start us, length us, event | category | flops | bytes accessed | tf_op | source)
XLA Modules:
  0.0 99.1 jit_solution(2236697985235903258)
XLA Ops:
  1.3 95.7 %shard_map.129 = (bf16[128,2560]{1,0:T(8,128)(2,1)}, f32[40,1024]{1,0:T(8,128)}, f32[40,128]{1,0:T(8,128)}, f32[40,128]{1,0:T(8,128)}) custom-call(bf16[128,2560]{1,0:T(8,128)(2,1)} %normed.1, bf16[2560,1024]{1,0:T(8,128)(2,1)} %w_query.1, bf16[2560,128]{1,0:T(8,128)(2,1)} %key_weight.1, bf16[2560,128]{1,0:T(8,128)(2,1)} %value_weight.1, f32[1,128]{1,0:T(1,128)} %bitcast.2, ...), custom_call_target="tpu_custom_call" | custom-call | tf_op jit(solution)/shard_map/pallas_call | solution.py:701
  97.0 2.1 %shard_map.130 = (bf16[128,2560]{1,0:T(8,128)(2,1)}, f32[40,1024]{1,0:T(8,128)}, f32[40,128]{1,0:T(8,128)}, f32[40,128]{1,0:T(8,128)}) custom-call(bf16[128,2560]{1,0:T(8,128)(2,1)} %get-tuple-element.8.refs_0_, f32[40,1024]{1,0:T(8,128)} %get-tuple-element.9.refs_1_, f32[40,128]{1,0:T(8,128)} %get-tuple-element.10.refs_2_, f32[40,128]{1,0:T(8,128)} %get-tuple-element.11.refs_3_), custom_call_target="tpu_custom_call" | custom-call | tf_op jit(solution)/shard_map/pallas_call | solution.py:722

commit v3 on v2

--- a/solution.py
+++ b/solution.py
@@ -28,16 +28,19 @@
 SCALE = HEAD**-0.5
 SCORE_SCALE = SCALE * math.log2(math.e)
 QUERY_ROWS = 256
-RINGED = (0, 2)
-STRAIGHT = (1, 3, 4)
+RINGED = (0, 1, 2, 3)
+STRAIGHT = (0, 1, 2, 3, 4)
+DIRECT = (4,)
+PADDED = 48
 
 GATHER = 0
 CONTEXT = GATHER + 6
 CORE = CONTEXT + 3 * (TILES - 1)
 RING_SLOT = CORE + TILES
-FINAL = RING_SLOT + 10 * TILES
-INPUT = FINAL + 1
-SLOTS = INPUT + 10
+DIRECT_SLOT = RING_SLOT + 10 * TILES
+FINAL = DIRECT_SLOT + 15 * len(DIRECT)
+INPUT = FINAL + TILES
+SLOTS = INPUT + 22
 
 
 def angle_tables():
@@ -78,7 +81,7 @@
     grads, dk_t, dv_t,
     part, part_send, part_recv, y_recv, z_send, z_recv,
     long_send, long_recv, short_send, short_recv, last_send, last_recv,
-    own_total, result, result_recv,
+    direct_send, direct_recv, own_total, result, result_recv,
     dx_far, dx_send_r, dx_send_l, dx_wait_r, dx_wait_l, dx_own,
     x_far_r, x_far_l, x_near_r, x_near_l,
     local_sem, send_sem, recv_sem,
@@ -97,7 +100,8 @@
     to_core = (place(y, z, 1 - core), x)
     partners = [to_xr, to_xl, to_xf, to_core]
     partners += [(place(lax.rem(y + k, RING_Y), z, core), x) for k in range(1, RING_Y)]
-    partners += [(place(y, lax.rem(z + k, RING_Z), core), x) for k in range(1, RING_Z)]
+    for core_at in (core, 1 - core):
+        partners += [(place(y, lax.rem(z + k, RING_Z), core_at), x) for k in range(1, RING_Z)]
 
     def remote(src, dst, slot, device):
         return pltpu.make_async_remote_copy(
@@ -191,7 +195,7 @@
                 queries_t[head, :, rows] = turned.T.astype(BF16)
             return carry
 
-        lax.fori_loop(0, HEADS // 2, pair, 0)
+        lax.fori_loop(0, HEADS // 2, pair, 0, unroll=True)
         out = dot(span[block], weights[:, QUERY_COLUMNS:])
         u = out[:, :HEAD]
         u_key[rows, :] = u
@@ -264,32 +268,27 @@
             target = rotated_rows((first + start) // ROWS)
             grads[target, columns] = low_values[start : start + ROWS]
 
-    def attend(head):
+    def attend(head, first):
         columns = pl.ds(aligned(head, HEAD), HEAD)
-        for first in range(0, SPAN, QUERY_ROWS):
-            rows = slice(first, first + QUERY_ROWS)
-            seen = first + QUERY_ROWS
-            position = lax.broadcasted_iota(jnp.int32, (QUERY_ROWS, 1), 0) + first
-            limit = jnp.minimum(position, length - 1)
-            key_position = lax.broadcasted_iota(jnp.int32, (QUERY_ROWS, seen), 1)
-            key, value = keys[:seen, :], values[:seen, :]
-            scores = dot_t(queries[head, rows, :], key)
-            weight = jnp.where(key_position <= limit, jnp.exp2(scores * SCORE_SCALE), 0.0)
-            probs = weight * (1.0 / jnp.sum(weight, -1, keepdims=True))
-            probs_low = probs.astype(BF16)
-            context = dot(probs_low, value)
-            d_out = jnp.where(position < length, ctx[rows, columns].astype(F32), 0.0)
-            d_low = d_out.astype(BF16)
-            delta = jnp.sum(d_out * context, -1, keepdims=True)
-            d_score = (probs * (dot_t(d_low, value) - delta)).astype(BF16)
-            d_query = dot(d_score, key) * SCALE
-            store_grads(
-                first,
-                columns,
-                norm_gradient(u_query[head, rows, :], q_gain[...], unrotated(d_query, rows)),
-            )
-            dk_t[:, :seen] += dot(queries_t[head, :, rows], d_score)
-            dv_t[:, :seen] += dot(d_out.T.astype(BF16), probs_low)
+        rows = slice(first, first + QUERY_ROWS)
+        seen = first + QUERY_ROWS
+        position = lax.broadcasted_iota(jnp.int32, (QUERY_ROWS, 1), 0) + first
+        limit = jnp.minimum(position, length - 1)
+        key_position = lax.broadcasted_iota(jnp.int32, (QUERY_ROWS, seen), 1)
+        key, value = keys[:seen, :], values[:seen, :]
+        d_out = jnp.where(position < length, ctx[rows, columns].astype(F32), 0.0)
+        scores = dot_t(queries[head, rows, :], key)
+        d_probs = dot_t(d_out.astype(BF16), value)
+        weight = jnp.where(key_position <= limit, jnp.exp2(scores * SCORE_SCALE), 0.0)
+        inverse = 1.0 / jnp.sum(weight, -1, keepdims=True)
+        delta = jnp.sum(weight * d_probs, -1, keepdims=True) * inverse
+        probs = weight * inverse
+        probs_low = probs.astype(BF16)
+        d_score = (probs * (d_probs - delta)).astype(BF16)
+        d_query = dot(d_score, key) * SCALE
+        gradient = norm_gradient(u_query[head, rows, :], q_gain[...], unrotated(d_query, rows))
+        store_grads(first, columns, gradient)
+        return dot(queries_t[head, :, rows], d_score), dot(d_out.T.astype(BF16), probs_low)
 
     dk_t[...] = jnp.zeros_like(dk_t)
     dv_t[...] = jnp.zeros_like(dv_t)
@@ -297,8 +296,11 @@
     def attend_pair(tile):
         for copy in context_copies(tile):
             copy.wait_recv()
-        for side in range(2):
-            attend(2 * tile + side)
+        for first in range(0, SPAN, QUERY_ROWS):
+            seen = first + QUERY_ROWS
+            sums = [attend(2 * tile + side, first) for side in range(2)]
+            dk_t[:, :seen] += sums[0][0] + sums[1][0]
+            dv_t[:, :seen] += sums[0][1] + sums[1][1]
 
     def key_value_gradients():
         d_key = dk_t[...].T * SCALE
@@ -310,7 +312,8 @@
         store_grads(0, slice(QUERY_COLUMNS + HEAD, COLUMNS), dv_t[...].T)
 
     half = ROWS // 2
-    sides = [pl.ds(0, FEATURES // 2), pl.ds(FEATURES // 2, FEATURES // 2)]
+    pieces = 5
+    sides = [pl.ds(i * FEATURES // pieces, FEATURES // pieces) for i in range(pieces)]
     far_copies, near_copies = [], []
     for i, side in enumerate(sides):
         far_copies += [
@@ -322,10 +325,10 @@
             remote(dx_send_l.at[high, side], x_near_l.at[high, side], INPUT + 4 * i + 3, to_xl),
         ]
     first_copies = [
-        remote(dx_send_r.at[high, :], x_near_r.at[high, :], INPUT + 8, to_xr),
-        remote(dx_send_l.at[low, :], x_near_l.at[low, :], INPUT + 9, to_xl),
+        remote(dx_send_r.at[high, :], x_near_r.at[high, :], INPUT + 4 * pieces, to_xr),
+        remote(dx_send_l.at[low, :], x_near_l.at[low, :], INPUT + 4 * pieces + 1, to_xl),
     ]
-    chunks = FEATURES // 512
+    chunks = FEATURES // (256 * pieces)
 
     def input_first(side):
         def chunk(i, carry):
@@ -342,7 +345,7 @@
         lax.fori_loop(side * chunks, (side + 1) * chunks, chunk, 0)
         for copy in far_copies[2 * side : 2 * side + 2]:
             copy.start()
-        if side == 1:
+        if side == pieces - 1:
             for copy in first_copies:
                 copy.start()
 
@@ -373,9 +376,12 @@
             ).astype(BF16)
             return carry
 
-        for copy in first_copies + near_copies:
+        for copy in first_copies:
             copy.wait_recv()
-        lax.fori_loop(0, FEATURES // 256, chunk, 0)
+        for side in range(pieces):
+            for copy in near_copies[2 * side : 2 * side + 2]:
+                copy.wait_recv()
+            lax.fori_loop(side * chunks, (side + 1) * chunks, chunk, 0)
 
     def core_copy(tile):
         return remote(part_send.at[tile], part_recv.at[tile], CORE + tile, to_core)
@@ -384,23 +390,25 @@
 
     def weight_gradient(tile):
         columns = pl.ds(aligned(tile, PAIR), PAIR)
-        by_z = lax.rem(tile + 1, 2) * (1 - lax.div(tile, 4))
-
-        def chunk(i, carry):
-            features = pl.ds(aligned(i, chunk_blocks * BLOCK_ROWS), chunk_blocks * BLOCK_ROWS)
-            out = dot(span_t[features, :], grads[:, columns])
-            kept = jnp.where(core == 0, out[:, :HEAD], out[:, HEAD:]).astype(BF16)
-            sent = jnp.where(core == 0, out[:, HEAD:], out[:, :HEAD]).astype(BF16)
-            for j in range(chunk_blocks):
-                block = chunk_blocks * i + j
-                block_z, block_y = lax.rem(block, RING_Z), lax.div(block, RING_Z)
-                at = by_z * (block_z * RING_Y + block_y) + (1 - by_z) * block
-                rows = slice(j * BLOCK_ROWS, (j + 1) * BLOCK_ROWS)
-                part[tile, at] = kept[rows]
-                part_send[tile, at] = sent[rows]
+        split = 1 - lax.div(tile, TILES - 1)
+
+        def place_of(block_y, block_z, by_z):
+            return by_z * (block_z * RING_Y + block_y) + (1 - by_z) * (block_y * RING_Z + block_z)
+
+        def chunk(block_y, carry):
+            size = chunk_blocks * BLOCK_ROWS
+            for first in range(0, RING_Z, chunk_blocks):
+                features = pl.ds(aligned(block_y * 2 + first // chunk_blocks, size), size)
+                out = dot(span_t[features, :], grads[:, columns])
+                kept = jnp.where(core == 0, out[:, :HEAD], out[:, HEAD:]).astype(BF16)
+                sent = jnp.where(core == 0, out[:, HEAD:], out[:, :HEAD]).astype(BF16)
+                for j in range(chunk_blocks):
+                    rows = slice(j * BLOCK_ROWS, (j + 1) * BLOCK_ROWS)
+                    part[tile, place_of(block_y, first + j, split * core)] = kept[rows]
+                    part_send[tile, place_of(block_y, first + j, split * (1 - core))] = sent[rows]
             return carry
 
-        lax.fori_loop(0, BLOCKS // chunk_blocks, chunk, 0)
+        lax.fori_loop(0, RING_Y, chunk, 0)
         core_copy(tile).start()
 
     def add_cores(tile):
@@ -413,9 +421,13 @@
         core_copy(tile).wait_recv()
         lax.fori_loop(0, BLOCKS // chunk_blocks, add, 0)
 
-    def store_result(tile, total):
-        result[0, tile] = total[:SHARE]
-        result[1, tile] = total[SHARE:]
+    def store_result(tile, mine, theirs):
+        if tile < TILES - 1:
+            gq_out[:, pl.ds(tile * PAIR + aligned(core, HEAD), HEAD)] = mine
+            gq_out[:, pl.ds(tile * PAIR + aligned(1 - core, HEAD), HEAD)] = theirs
+        else:
+            gk_out[...] = jnp.where(core == 0, mine, theirs)
+            gv_out[...] = jnp.where(core == 0, theirs, mine)
 
     def y_copies(tile):
         slot = RING_SLOT + 10 * tile
@@ -448,42 +460,86 @@
         for copy in y_copies(tile):
             copy.start()
 
+    def final_copy(tile):
+        return remote(result.at[1 - core, tile], result_recv.at[tile], FINAL + tile, to_core)
+
+    def direct_copies(tile):
+        index = DIRECT.index(tile)
+        copies = []
+        for k in range(RING_Z):
+            for other in (0, 1):
+                if k or other:
+                    core_at = core if other == 0 else 1 - core
+                    copies.append(
+                        remote(
+                            direct_send.at[index, k, core_at],
+                            direct_recv.at[index, core, k],
+                            DIRECT_SLOT + 15 * index + 2 * k + other - 1,
+                            (place(y, lax.rem(z + k, RING_Z), core_at), x),
+                        )
+                    )
+        return copies
+
     def straight_second(tile):
         index = STRAIGHT.index(tile)
         for copy in y_copies(tile):
             copy.wait_recv()
-        copies = z_copies(tile)
+        direct = tile in DIRECT
+        copies = direct_copies(tile) if direct else z_copies(tile)
         for k in (1, 2, 3, 4, 5, 6, 7, 0):
             block = lax.rem(z + k, RING_Z)
             total = part[tile, y * RING_Z + block].astype(F32)
             for i in range(3):
                 total = total + y_recv[index, i, block].astype(F32)
-            if k:
+            if k == 0:
+                own_total[tile, 0] = total[:SHARE]
+                own_total[tile, 1] = total[SHARE:]
+            elif not direct:
                 z_send[index, k - 1] = total.astype(BF16)
                 copies[k - 1].start()
-            else:
-                own_total[tile] = total
+            if direct:
+                at = DIRECT.index(tile)
+                padding = jnp.zeros((PADDED - SHARE, HEAD), F32)
+                for side in (0, 1):
+                    rows = total[side * SHARE : (side + 1) * SHARE]
+                    direct_send[at, k, side] = jnp.concatenate([rows, padding]).astype(BF16)
+                for copy in copies[2 * k - 1 : 2 * k + 1] if k else copies[:1]:
+                    copy.start()
 
     def straight_third(tile):
         index = STRAIGHT.index(tile)
+        if tile in DIRECT:
+            at = DIRECT.index(tile)
+            for copy in direct_copies(tile):
+                copy.wait_recv()
+            mine = own_total[tile, core]
+            for i in range(1, RING_Z):
+                mine = mine + direct_recv[at, core, i].astype(F32)[:SHARE]
+            theirs = direct_recv[at, 1 - core, 0].astype(F32)[:SHARE]
+            for i in range(1, RING_Z):
+                theirs = theirs + direct_recv[at, 1 - core, i].astype(F32)[:SHARE]
+            store_result(tile, mine, theirs)
+            return
         for copy in z_copies(tile):
             copy.wait_recv()
-        total = own_total[tile]
-        for i in range(RING_Z - 1):
-            total = total + z_recv[index, i].astype(F32)
-        store_result(tile, total)
-
-    sign = 1 - 2 * core
-
-    def ahead(k):
-        return lax.rem(z + RING_Z + sign * k, RING_Z)
-
-    to_long, to_short = (place(y, ahead(1), core), x), (place(y, ahead(-1), core), x)
+        for side in (0, 1):
+            rows = slice(side * SHARE, (side + 1) * SHARE)
+            total = own_total[tile, side]
+            for i in range(RING_Z - 1):
+                total = total + z_recv[index, i].astype(F32)[rows]
+            result[side, tile] = total
+        final_copy(tile).start()
+
+    def ahead(tile, k):
+        return lax.rem(z + RING_Z + (k if tile % 2 else -k), RING_Z)
 
     def long_copy(tile, step):
         index = RINGED.index(tile)
         return remote(
-            long_send.at[index, step], long_recv.at[index, step], RING_SLOT + 10 * tile + step, to_long
+            long_send.at[index, step],
+            long_recv.at[index, step],
+            RING_SLOT + 10 * tile + step,
+            (place(y, ahead(tile, 1), core), x),
         )
 
     def short_copy(tile, step):
@@ -492,7 +548,7 @@
             short_send.at[index, step],
             short_recv.at[index, step],
             RING_SLOT + 10 * tile + 4 + step,
-            to_short,
+            (place(y, ahead(tile, -1), core), x),
         )
 
     def ring_part(tile, block):
@@ -502,14 +558,14 @@
         index = RINGED.index(tile)
         if step == 0:
             add_cores(tile)
-        total = ring_part(tile, ahead(4 - step))
+        total = ring_part(tile, ahead(tile, 4 - step))
         if step > 0:
             long_copy(tile, step - 1).wait_recv()
             total = total + long_recv[index, step - 1].astype(F32)
         long_send[index, step] = total.astype(BF16)
         long_copy(tile, step).start()
         if step < 3:
-            total = ring_part(tile, ahead(step - 3))
+            total = ring_part(tile, ahead(tile, step - 3))
             if step > 0:
                 short_copy(tile, step - 1).wait_recv()
                 total = total + short_recv[index, step - 1].astype(F32)
@@ -544,16 +600,34 @@
                 last_send[index, k - 1] = total.astype(BF16)
                 copies[k - 1].start()
             else:
-                own_total[tile] = total
+                own_total[tile, 0] = total[:SHARE]
+                own_total[tile, 1] = total[SHARE:]
 
     def ring_sixth(tile):
         index = RINGED.index(tile)
         for copy in last_copies(tile):
             copy.wait_recv()
-        total = own_total[tile]
-        for i in range(3):
-            total = total + last_recv[index, i].astype(F32)
-        store_result(tile, total)
+        for side in (0, 1):
+            rows = slice(side * SHARE, (side + 1) * SHARE)
+            total = own_total[tile, side]
+            for i in range(3):
+                total = total + last_recv[index, i].astype(F32)[rows]
+            result[side, tile] = total
+        final_copy(tile).start()
+
+    def on_cores(straight, ringed):
+        @pl.when(core == 0)
+        def _():
+            for stage, tile in straight:
+                (straight_first, straight_second, straight_third)[stage](tile)
+
+        @pl.when(core == 1)
+        def _():
+            for stage, tile in ringed:
+                if stage < 4:
+                    ring_step(tile, stage)
+                else:
+                    (ring_fifth, ring_sixth)[stage - 4](tile)
 
     def step(turn, carry):
         attend_pair(turn)
@@ -562,58 +636,44 @@
         def _():
             weight_gradient(turn)
 
-        @pl.when(turn == 1)
-        def _():
-            ring_step(0, 0)
-
-        @pl.when(turn == 2)
-        def _():
-            straight_first(1)
-            ring_step(0, 1)
+        for tile in (0, 1):
+
+            @pl.when(turn == tile + 1)
+            def _(tile=tile):
+                on_cores([(0, tile)], [(0, tile)])
 
         return carry
 
     lax.fori_loop(0, TILES - 1, step, 0)
+    weight_gradient(3)
+    on_cores([(0, 2), (1, 0)], [(0, 2), (1, 0), (1, 1)])
     key_value_gradients()
     input_first(0)
-    weight_gradient(3)
     weight_gradient(4)
     input_first(1)
-    ring_step(2, 0)
-    ring_step(0, 2)
-    straight_first(3)
+    on_cores([(0, 3)], [(0, 3)])
+    input_first(2)
+    input_first(3)
     straight_first(4)
-    straight_second(1)
-    ring_step(2, 1)
-    ring_step(0, 3)
+    input_first(4)
+    on_cores([(1, 1), (1, 2), (2, 0)], [(2, 0), (2, 1), (1, 2), (1, 3)])
     input_second(0)
-    ring_step(2, 2)
-    straight_third(1)
-    ring_fifth(0)
     input_second(1)
-    ring_step(2, 3)
-    straight_second(3)
-    ring_sixth(0)
-    ring_fifth(2)
+    input_second(2)
+    on_cores([(1, 3), (2, 1)], [(3, 0), (3, 1), (2, 2), (2, 3)])
+    input_second(3)
+    input_second(4)
+    on_cores([(2, 2)], [(4, 0), (4, 1), (3, 2), (3, 3)])
     straight_second(4)
-    straight_third(3)
-    ring_sixth(2)
+    on_cores([(2, 3)], [(5, 0), (5, 1), (4, 2), (4, 3), (5, 2), (5, 3)])
+    for tile in range(TILES):
+        if tile not in DIRECT:
+            final_copy(tile).wait_recv()
+            store_result(tile, result[core, tile], result_recv[tile])
     straight_third(4)
-
-    final = remote(result.at[1 - core], result_recv, FINAL, to_core)
-    final.start()
     input_last()
-    final.wait_recv()
-
-    mine, other = aligned(core, HEAD), aligned(1 - core, HEAD)
-    for tile in range(TILES - 1):
-        gq_out[:, pl.ds(tile * PAIR + mine, HEAD)] = result[core, tile]
-        gq_out[:, pl.ds(tile * PAIR + other, HEAD)] = result_recv[tile]
-    kept, received = result[core, TILES - 1], result_recv[TILES - 1]
-    gk_out[...] = jnp.where(core == 0, kept, received)
-    gv_out[...] = jnp.where(core == 0, received, kept)
-
-    for copy in (right_low, right_high, left_high, left_low, pass_right, pass_left, final):
+
+    for copy in (right_low, right_high, left_high, left_low, pass_right, pass_left):
         copy.wait_send()
     for copy in far_copies + near_copies + first_copies:
         copy.wait_send()
@@ -624,15 +684,26 @@
         return carry
 
     lax.fori_loop(0, TILES - 1, drain_context, 0)
-    for tile in range(TILES):
-        copies = [core_copy(tile)]
-        if tile in RINGED:
-            copies += [long_copy(tile, i) for i in range(4)] + [short_copy(tile, i) for i in range(3)]
-            copies += last_copies(tile)
-        else:
-            copies += y_copies(tile) + z_copies(tile)
+    def finish(copies):
         for copy in copies:
             copy.wait_send()
+
+    for tile in range(TILES):
+        finish([core_copy(tile)])
+        if tile in DIRECT:
+            finish(y_copies(tile) + direct_copies(tile))
+        else:
+            finish([final_copy(tile)])
+
+            @pl.when(core == 0)
+            def _(tile=tile):
+                finish(y_copies(tile) + z_copies(tile))
+
+            @pl.when(core == 1)
+            def _(tile=tile):
+                finish([long_copy(tile, i) for i in range(4)])
+                finish([short_copy(tile, i) for i in range(3)])
+                finish(last_copies(tile))
 
 
 def write_results(*refs):
@@ -675,7 +746,9 @@
         pltpu.VMEM((len(RINGED), 3, RING_Y) + block, BF16),
         pltpu.VMEM((len(RINGED), 3) + block, BF16),
         pltpu.VMEM((len(RINGED), 3) + block, BF16),
-        pltpu.VMEM((TILES,) + block, F32),
+        pltpu.VMEM((len(DIRECT), RING_Z, 2, PADDED, HEAD), BF16),
+        pltpu.VMEM((len(DIRECT), 2, RING_Z, PADDED, HEAD), BF16),
+        pltpu.VMEM((TILES, 2, SHARE, HEAD), F32),
         pltpu.VMEM((2, TILES, SHARE, HEAD), F32),
         pltpu.VMEM((TILES, SHARE, HEAD), F32),
         pltpu.VMEM((ROWS, FEATURES), BF16),

time: 99.2 us -> 87.4 us (0.88)
  Pallas kernels: 97.8 us -> 86 us
    pallas_call x1, Pallas kernels: 95.7 us -> 83.9 us  [local(): pl.pallas_call(kernel, out_shape=out_shape, in_specs=[anywhere] * 4 + [vm...]
where the time goes in v3:
time: 87.4 us; the launch traced here: 87.3 us
  Pallas kernels  86 us (98%)
  between operations  1.29 us (1%)
    pallas_call x1, Pallas kernels, local(): pl.pallas_call(kernel, out_shape=out_shape, in_specs=[anywhere] * 4 + [vm...  83.9 us
    pallas_call x1, Pallas kernels, local(): pl.pallas_call(write_results, out_shape=out_shape, in_specs=[vmem] * 4, o...  2.09 us

profile of v3, /device:TPU:1, one launch (start us, length us, event | category | flops | bytes accessed | tf_op | source)
XLA Modules:
  0.0 87.3 jit_solution(12837959036960049697)
XLA Ops:
  1.3 83.9 %shard_map.129 = (bf16[128,2560]{1,0:T(8,128)(2,1)}, f32[40,1024]{1,0:T(8,128)}, f32[40,128]{1,0:T(8,128)}, f32[40,128]{1,0:T(8,128)}) custom-call(bf16[128,2560]{1,0:T(8,128)(2,1)} %normed.1, bf16[2560,1024]{1,0:T(8,128)(2,1)} %w_query.1, bf16[2560,128]{1,0:T(8,128)(2,1)} %key_weight.1, bf16[2560,128]{1,0:T(8,128)(2,1)} %value_weight.1, f32[1,128]{1,0:T(1,128)} %bitcast.2, ...), custom_call_target="tpu_custom_call" | custom-call | tf_op jit(solution)/shard_map/pallas_call | solution.py:774
  85.2 2.1 %shard_map.130 = (bf16[128,2560]{1,0:T(8,128)(2,1)}, f32[40,1024]{1,0:T(8,128)}, f32[40,128]{1,0:T(8,128)}, f32[40,128]{1,0:T(8,128)}) custom-call(bf16[128,2560]{1,0:T(8,128)(2,1)} %get-tuple-element.8.refs_0_, f32[40,1024]{1,0:T(8,128)} %get-tuple-element.9.refs_1_, f32[40,128]{1,0:T(8,128)} %get-tuple-element.10.refs_2_, f32[40,128]{1,0:T(8,128)} %get-tuple-element.11.refs_3_), custom_call_target="tpu_custom_call" | custom-call | tf_op jit(solution)/shard_map/pallas_call | solution.py:795

commit v4 on v3

--- a/solution.py
+++ b/solution.py
@@ -76,7 +76,7 @@
 
 def kernel(
     normed, w_query, key_weight, value_weight, q_gain, k_gain, ctx_in, lengths, cosine_in, sine_in,
-    dx_out, gq_out, gk_out, gv_out,
+    dx_hbm, gq_hbm, gk_hbm, gv_hbm, dx_out, gq_out, gk_out, gv_out,
     cosine, sine, weights, weights_t, span, span_t, ctx, u_query, u_key, queries, queries_t, keys, values,
     grads, dk_t, dv_t,
     part, part_send, part_recv, y_recv, z_send, z_recv,
@@ -314,6 +314,13 @@
     half = ROWS // 2
     pieces = 5
     sides = [pl.ds(i * FEATURES // pieces, FEATURES // pieces) for i in range(pieces)]
+    stores = [
+        pltpu.make_async_copy(source, target, local_sem.at[7 + i])
+        for i, (source, target) in enumerate(
+            [(gq_out, gq_hbm), (gk_out, gk_hbm), (gv_out, gv_hbm)]
+            + [(dx_out.at[:, side], dx_hbm.at[:, side]) for side in sides]
+        )
+    ]
     far_copies, near_copies = [], []
     for i, side in enumerate(sides):
         far_copies += [
@@ -342,7 +349,7 @@
             dx_send_r[half:, features] = out[2 * ROWS + half : 3 * ROWS].astype(BF16)
             return carry
 
-        lax.fori_loop(side * chunks, (side + 1) * chunks, chunk, 0)
+        lax.fori_loop(side * chunks, (side + 1) * chunks, chunk, 0, unroll=True)
         for copy in far_copies[2 * side : 2 * side + 2]:
             copy.start()
         if side == pieces - 1:
@@ -382,6 +389,7 @@
             for copy in near_copies[2 * side : 2 * side + 2]:
                 copy.wait_recv()
             lax.fori_loop(side * chunks, (side + 1) * chunks, chunk, 0)
+            stores[3 + side].start()
 
     def core_copy(tile):
         return remote(part_send.at[tile], part_recv.at[tile], CORE + tile, to_core)
@@ -408,7 +416,7 @@
                     part_send[tile, place_of(block_y, first + j, split * (1 - core))] = sent[rows]
             return carry
 
-        lax.fori_loop(0, RING_Y, chunk, 0)
+        lax.fori_loop(0, RING_Y, chunk, 0, unroll=True)
         core_copy(tile).start()
 
     def add_cores(tile):
@@ -419,7 +427,7 @@
             return carry
 
         core_copy(tile).wait_recv()
-        lax.fori_loop(0, BLOCKS // chunk_blocks, add, 0)
+        lax.fori_loop(0, BLOCKS // chunk_blocks, add, 0, unroll=2)
 
     def store_result(tile, mine, theirs):
         if tile < TILES - 1:
@@ -615,6 +623,32 @@
             result[side, tile] = total
         final_copy(tile).start()
 
+    def finish(copies):
+        for copy in copies:
+            copy.wait_send()
+
+    def finish_tile(tile):
+        if tile in DIRECT:
+            finish(y_copies(tile) + direct_copies(tile))
+            return
+        finish([final_copy(tile)])
+
+        @pl.when(core == 0)
+        def _():
+            finish(y_copies(tile) + z_copies(tile))
+
+        @pl.when(core == 1)
+        def _():
+            finish([long_copy(tile, i) for i in range(4)])
+            finish([short_copy(tile, i) for i in range(3)])
+            finish(last_copies(tile))
+
+    def finish_first():
+        finish([right_low, right_high, left_high, left_low, pass_right, pass_left])
+        for tile in range(TILES - 1):
+            finish(context_copies(tile))
+        finish(far_copies)
+
     def on_cores(straight, ringed):
         @pl.when(core == 0)
         def _():
@@ -648,8 +682,8 @@
     weight_gradient(3)
     on_cores([(0, 2), (1, 0)], [(0, 2), (1, 0), (1, 1)])
     key_value_gradients()
+    weight_gradient(4)
     input_first(0)
-    weight_gradient(4)
     input_first(1)
     on_cores([(0, 3)], [(0, 3)])
     input_first(2)
@@ -671,39 +705,18 @@
             final_copy(tile).wait_recv()
             store_result(tile, result[core, tile], result_recv[tile])
     straight_third(4)
+    for copy in stores[:3]:
+        copy.start()
     input_last()
 
-    for copy in (right_low, right_high, left_high, left_low, pass_right, pass_left):
-        copy.wait_send()
-    for copy in far_copies + near_copies + first_copies:
-        copy.wait_send()
-
-    def drain_context(tile, carry):
-        for copy in context_copies(tile):
-            copy.wait_send()
-        return carry
-
-    lax.fori_loop(0, TILES - 1, drain_context, 0)
-    def finish(copies):
-        for copy in copies:
-            copy.wait_send()
-
+    finish_first()
+    finish([core_copy(tile) for tile in range(TILES)])
+    finish(first_copies)
+    finish(near_copies)
     for tile in range(TILES):
-        finish([core_copy(tile)])
-        if tile in DIRECT:
-            finish(y_copies(tile) + direct_copies(tile))
-        else:
-            finish([final_copy(tile)])
-
-            @pl.when(core == 0)
-            def _(tile=tile):
-                finish(y_copies(tile) + z_copies(tile))
-
-            @pl.when(core == 1)
-            def _(tile=tile):
-                finish([long_copy(tile, i) for i in range(4)])
-                finish([short_copy(tile, i) for i in range(3)])
-                finish(last_copies(tile))
+        finish_tile(tile)
+    for copy in stores:
+        copy.wait()
 
 
 def write_results(*refs):
@@ -718,6 +731,10 @@
     anywhere = pl.BlockSpec(memory_space=pl.ANY)
     smem = pl.BlockSpec(memory_space=pltpu.SMEM)
     scratch = [
+        pltpu.VMEM((ROWS, FEATURES), BF16),
+        pltpu.VMEM((SHARE, QUERY_COLUMNS), F32),
+        pltpu.VMEM((SHARE, HEAD), F32),
+        pltpu.VMEM((SHARE, HEAD), F32),
         pltpu.VMEM((SPAN, HEAD), F32),
         pltpu.VMEM((SPAN, HEAD), F32),
         pltpu.VMEM((FEATURES, COLUMNS), BF16),
@@ -761,7 +778,7 @@
         pltpu.VMEM((ROWS // 2, FEATURES), BF16),
         pltpu.VMEM((ROWS, FEATURES), BF16),
         pltpu.VMEM((ROWS, FEATURES), BF16),
-        pltpu.SemaphoreType.DMA((7,)),
+        pltpu.SemaphoreType.DMA((15,)),
         pltpu.SemaphoreType.DMA((SLOTS,)),
         pltpu.SemaphoreType.DMA((SLOTS,)),
     ]
@@ -775,7 +792,7 @@
         kernel,
         out_shape=out_shape,
         in_specs=[anywhere] * 4 + [vmem] * 2 + [anywhere, smem, anywhere, anywhere],
-        out_specs=(vmem,) * 4,
+        out_specs=(anywhere,) * 4,
         scratch_shapes=scratch,
         compiler_params=pltpu.CompilerParams(
             collective_id=0, has_side_effects=True, vmem_limit_bytes=60 * 2**20

time: 87.4 us -> 84 us (0.961)
  Pallas kernels: 86 us -> 81.8 us
    pallas_call x1, Pallas kernels: 83.9 us -> 79.7 us  [local(): pl.pallas_call(kernel, out_shape=out_shape, in_specs=[anywhere] * 4 + [vm...]
where the time goes in v4:
time: 84 us; the launch traced here: 83.1 us
  Pallas kernels  81.8 us (97%)
  between operations  1.29 us (2%)
    pallas_call x1, Pallas kernels, local(): pl.pallas_call(kernel, out_shape=out_shape, in_specs=[anywhere] * 4 + [vm...  79.7 us
    pallas_call x1, Pallas kernels, local(): pl.pallas_call(write_results, out_shape=out_shape, in_specs=[vmem] * 4, o...  2.09 us

profile of v4, /device:TPU:1, one launch (start us, length us, event | category | flops | bytes accessed | tf_op | source)
XLA Modules:
  0.0 83.1 jit_solution(15581430767876135235)
XLA Ops:
  1.3 79.7 %shard_map.129 = (bf16[128,2560]{1,0:T(8,128)(2,1)}, f32[40,1024]{1,0:T(8,128)}, f32[40,128]{1,0:T(8,128)}, f32[40,128]{1,0:T(8,128)}) custom-call(bf16[128,2560]{1,0:T(8,128)(2,1)} %normed.1, bf16[2560,1024]{1,0:T(8,128)(2,1)} %w_query.1, bf16[2560,128]{1,0:T(8,128)(2,1)} %key_weight.1, bf16[2560,128]{1,0:T(8,128)(2,1)} %value_weight.1, f32[1,128]{1,0:T(1,128)} %bitcast.2, ...), custom_call_target="tpu_custom_call" | custom-call | tf_op jit(solution)/shard_map/pallas_call | solution.py:791
  81.0 2.1 %shard_map.130 = (bf16[128,2560]{1,0:T(8,128)(2,1)}, f32[40,1024]{1,0:T(8,128)}, f32[40,128]{1,0:T(8,128)}, f32[40,128]{1,0:T(8,128)}) custom-call(bf16[128,2560]{1,0:T(8,128)(2,1)} %get-tuple-element.8.refs_0_, f32[40,1024]{1,0:T(8,128)} %get-tuple-element.9.refs_1_, f32[40,128]{1,0:T(8,128)} %get-tuple-element.10.refs_2_, f32[40,128]{1,0:T(8,128)} %get-tuple-element.11.refs_3_), custom_call_target="tpu_custom_call" | custom-call | tf_op jit(solution)/shard_map/pallas_call | solution.py:812

commit v5 on v4

--- a/solution.py
+++ b/solution.py
@@ -211,7 +211,7 @@
             span_t[features, rotated_rows(block)] = span[block, :, features].T
             return carry
 
-        lax.fori_loop(0, FEATURES // 256, chunk, 0)
+        lax.fori_loop(0, FEATURES // 256, chunk, 0, unroll=5)
 
     def transpose_weights():
         def chunk(i, carry):
@@ -369,7 +369,7 @@
 
         for copy in far_copies[2 * side : 2 * side + 2]:
             copy.wait_recv()
-        lax.fori_loop(side * chunks, (side + 1) * chunks, chunk, 0)
+        lax.fori_loop(side * chunks, (side + 1) * chunks, chunk, 0, unroll=True)
         for copy in near_copies[2 * side : 2 * side + 2]:
             copy.start()
 
@@ -388,7 +388,7 @@
         for side in range(pieces):
             for copy in near_copies[2 * side : 2 * side + 2]:
                 copy.wait_recv()
-            lax.fori_loop(side * chunks, (side + 1) * chunks, chunk, 0)
+            lax.fori_loop(side * chunks, (side + 1) * chunks, chunk, 0, unroll=True)
             stores[3 + side].start()
 
     def core_copy(tile):
@@ -427,7 +427,7 @@
             return carry
 
         core_copy(tile).wait_recv()
-        lax.fori_loop(0, BLOCKS // chunk_blocks, add, 0, unroll=2)
+        lax.fori_loop(0, BLOCKS // chunk_blocks, add, 0, unroll=4)
 
     def store_result(tile, mine, theirs):
         if tile < TILES - 1:

time: 84 us -> 83.8 us (level)
  no operation moved by 1% of the time
where the time goes in v5:
time: 83.8 us; the launch traced here: 83.5 us
  Pallas kernels  82.2 us (98%)
  between operations  1.29 us (2%)
    pallas_call x1, Pallas kernels, local(): pl.pallas_call(kernel, out_shape=out_shape, in_specs=[anywhere] * 4 + [vm...  80.1 us
    pallas_call x1, Pallas kernels, local(): pl.pallas_call(write_results, out_shape=out_shape, in_specs=[vmem] * 4, o...  2.09 us

profile of v5, /device:TPU:1, one launch (start us, length us, event | category | flops | bytes accessed | tf_op | source)
XLA Modules:
  0.0 83.5 jit_solution(1598314593242373359)
XLA Ops:
  1.3 80.1 %shard_map.129 = (bf16[128,2560]{1,0:T(8,128)(2,1)}, f32[40,1024]{1,0:T(8,128)}, f32[40,128]{1,0:T(8,128)}, f32[40,128]{1,0:T(8,128)}) custom-call(bf16[128,2560]{1,0:T(8,128)(2,1)} %normed.1, bf16[2560,1024]{1,0:T(8,128)(2,1)} %w_query.1, bf16[2560,128]{1,0:T(8,128)(2,1)} %key_weight.1, bf16[2560,128]{1,0:T(8,128)(2,1)} %value_weight.1, f32[1,128]{1,0:T(1,128)} %bitcast.2, ...), custom_call_target="tpu_custom_call" | custom-call | tf_op jit(solution)/shard_map/pallas_call | solution.py:791
  81.4 2.1 %shard_map.130 = (bf16[128,2560]{1,0:T(8,128)(2,1)}, f32[40,1024]{1,0:T(8,128)}, f32[40,128]{1,0:T(8,128)}, f32[40,128]{1,0:T(8,128)}) custom-call(bf16[128,2560]{1,0:T(8,128)(2,1)} %get-tuple-element.8.refs_0_, f32[40,1024]{1,0:T(8,128)} %get-tuple-element.9.refs_1_, f32[40,128]{1,0:T(8,128)} %get-tuple-element.10.refs_2_, f32[40,128]{1,0:T(8,128)} %get-tuple-element.11.refs_3_), custom_call_target="tpu_custom_call" | custom-call | tf_op jit(solution)/shard_map/pallas_call | solution.py:812
